TPU v7x, 256 devices: a whole 4x4x8 slice. The times are simulated.
256 devices in a mesh: ens: 32 (over x, y, core), bal: 8 (over z).
Axes of the slice: x: 4, y: 4, z: 8, core: 2. Of those that a mesh axis runs over, the one named last changes fastest.
Arguments:
- members: float32 [256, 1024, 4, 128], P('ens', 'bal'), may hold values from -6 to 6
- obs_ens: bfloat16 [256, 1024, 2048], P('ens', 'bal'), may hold values from -16 to 16
- obs_count: int32 [1024], replicated, may hold values from 0 to 2048, as said below
- obs_value: float32 [1024, 2048], P(('bal', 'ens')), may hold values from -6 to 6
- obs_weight: float32 [1024, 2048], P(('bal', 'ens')), may hold values from 0.02 to 0.5
Outputs:
- analysis: float32 [256, 1024, 4, 128], P('ens', 'bal')
Inputs may be any that keep to these rules, and one draw needn't show every extreme that they name: `obs_count`: some tile has all 2048 slots live and some tile has none.
All inputs are finite; a program needn't handle non-finite values.
Results may differ from a plain program's by a relative error of at most 0.0031.
Values may be sent and summed in bfloat16 or wider, within the bound.
A program may use at most 64 MiB of HBM per device.

v0:
```python
import jax
import jax.numpy as jnp
from jax import lax
from jax.sharding import PartitionSpec as P

NEWTON = 5


def solve_weights(gram_matrix, obs_vector):
    highest = lax.Precision.HIGHEST
    ens_size = gram_matrix.shape[0]
    identity = jnp.eye(ens_size, dtype=jnp.float32)
    scale_bound = ens_size - 1.0 + jnp.trace(gram_matrix)
    y_matrix = ((ens_size - 1.0) * identity + gram_matrix) / scale_bound
    z_matrix = identity
    for iteration in range(NEWTON):
        middle = 1.5 * identity - 0.5 * jnp.dot(z_matrix, y_matrix, precision=highest)
        y_matrix = jnp.dot(y_matrix, middle, precision=highest)
        z_matrix = jnp.dot(middle, z_matrix, precision=highest)
    inner_vec = jnp.dot(z_matrix, obs_vector, precision=highest)
    shift_vec = jnp.dot(z_matrix, inner_vec, precision=highest) / scale_bound
    factor = jnp.sqrt(ens_size - 1.0) / jnp.sqrt(scale_bound)
    return (factor * z_matrix + shift_vec[:, None]).astype(jnp.bfloat16)


def unit_weights(gram_matrix, obs_vector):
    return jnp.eye(gram_matrix.shape[0], dtype=jnp.bfloat16)


def tile_weights(operands):
    gram_matrix, obs_vector = operands
    return lax.cond(
        jnp.trace(gram_matrix) > 0.0, solve_weights, unit_weights, gram_matrix, obs_vector
    )


def tile_gram(obs_rows, centre_row, weight_row, innov_row, live_count, ens_size):
    zero_sums = (jnp.zeros((ens_size, ens_size), jnp.float32), jnp.zeros((ens_size,), jnp.float32))
    block_count = (live_count + 127) // 128

    def add_block(index_block, totals):
        first_slot = index_block * 128
        obs_piece = lax.dynamic_slice_in_dim(obs_rows, first_slot, 128, 1)
        centre_piece = lax.dynamic_slice_in_dim(centre_row, first_slot, 128, 0)
        weight_piece = lax.dynamic_slice_in_dim(weight_row, first_slot, 128, 0)
        rhs_piece = lax.dynamic_slice_in_dim(innov_row, first_slot, 128, 0)
        root_piece = (
            weight_piece[None, :] * (obs_piece.astype(jnp.float32) - centre_piece[None, :])
        ).astype(jnp.bfloat16)
        gram_piece = lax.dot_general(
            root_piece, root_piece, (((1,), (1,)), ((), ())), preferred_element_type=jnp.float32
        )
        vector_piece = jnp.dot(root_piece, rhs_piece, preferred_element_type=jnp.float32)
        return (totals[0] + gram_piece, totals[1] + vector_piece)

    return lax.fori_loop(0, block_count, add_block, zero_sums)


def body(members, obs_ens, obs_count, obs_value, obs_weight):
    member_block, tile_block, nfield, columns = members.shape
    ens_ways = lax.axis_size("ens")
    ens_size = member_block * ens_ways
    per_device, slot_count = obs_value.shape
    state_width = nfield * columns
    first_tile = (lax.axis_index("bal") * ens_ways + lax.axis_index("ens")) * per_device
    ensemble = lax.all_to_all(members, "ens", split_axis=1, concat_axis=0, tiled=True)
    observed = lax.all_to_all(obs_ens, "ens", split_axis=1, concat_axis=0, tiled=True)
    mean_tiles = jnp.mean(ensemble, axis=0)
    pert_tiles = (ensemble - mean_tiles[None]).astype(jnp.bfloat16)
    pert_tiles = pert_tiles.reshape(ens_size, per_device, state_width)
    mean_tiles = mean_tiles.reshape(per_device, state_width)
    obs_mean = jnp.sum(observed, axis=0, dtype=jnp.float32) / ens_size
    counts = lax.dynamic_slice_in_dim(obs_count, first_tile, per_device, 0)
    positions = lax.broadcasted_iota(jnp.int32, (per_device, slot_count), 1)
    live_mask = positions < counts[:, None]
    innovation = jnp.where(live_mask, obs_value - obs_mean, 0.0)
    root_weight = jnp.sqrt(obs_weight)
    masked_weight = jnp.where(live_mask, root_weight, 0.0)
    scaled_innov = (root_weight * innovation).astype(jnp.bfloat16)
    grams = []
    vectors = []
    for tile_index in range(per_device):
        gram_one, vector_one = tile_gram(
            observed[:, tile_index],
            obs_mean[tile_index],
            masked_weight[tile_index],
            scaled_innov[tile_index],
            counts[tile_index],
            ens_size,
        )
        grams.append(gram_one)
        vectors.append(vector_one)
    gram_tiles = jnp.stack(grams)
    vector_tiles = jnp.stack(vectors)
    weights = lax.map(tile_weights, (gram_tiles, vector_tiles))
    result = mean_tiles[None] + jnp.einsum(
        "tjk,jtf->ktf", weights, pert_tiles, preferred_element_type=jnp.float32
    )
    result = result.reshape(ens_size, per_device, nfield, columns)
    return lax.all_to_all(result, "ens", split_axis=0, concat_axis=1, tiled=True)


def solution(mesh):
    in_specs = (
        P("ens", "bal", None, None),
        P("ens", "bal", None),
        P(),
        P(("bal", "ens"), None),
        P(("bal", "ens"), None),
    )
    out_specs = P("ens", "bal", None, None)
    return jax.shard_map(body, mesh=mesh, in_specs=in_specs, out_specs=out_specs, check_vma=False)
```

profile of v0, /device:TPU:129, one launch (start us, length us, event | category | flops | bytes accessed | tf_op | source)
XLA Modules:
  0.0 249.1 jit_solution(16750990893064370763)
XLA Ops:
  0.0 3.5 %copy.19 = f32[8,128,4,128]{3,2,0,1:T(4,128)} copy(f32[8,128,4,128]{3,2,1,0:T(4,128)} %param.17) | data formatting | bytes 4194304 | tf_op args[0]
  3.5 7.8 %all-to-all-start = ((f32[8,128,4,128]{3,2,0,1:T(4,128)}), f32[8,128,4,128]{3,2,0,1:T(4,128)S(1)}, u32[]{:S(2)}, u32[]{:S(2)}) async-start(f32[8,128,4,128]{3,2,0,1:T(4,128)} %copy.19), calls=%async_computation | async-start | bytes 4194304 | tf_op jit(solution)/shard_map/all_to_all | solution.py:66
  11.3 6.5 %copy.21 = bf16[8,128,2048]{2,0,1:T(8,128)(2,1)} copy(bf16[8,128,2048]{2,1,0:T(8,128)(2,1)} %param.18) | data formatting | bytes 8388608 | tf_op args[1]
  17.7 21.8 %all-to-all-done = f32[8,128,4,128]{3,2,0,1:T(4,128)S(1)} async-done(((f32[8,128,4,128]{3,2,0,1:T(4,128)}), f32[8,128,4,128]{3,2,0,1:T(4,128)S(1)}, u32[]{:S(2)}, u32[]{:S(2)}) %all-to-all-start) | async-done | bytes 2097184 | tf_op jit(solution)/shard_map/all_to_all | solution.py:66
  39.6 5.3 %all-to-all-start.1 = ((bf16[8,128,2048]{2,0,1:T(8,128)(2,1)}), bf16[8,128,2048]{2,0,1:T(8,128)(2,1)}, u32[]{:S(2)}, u32[]{:S(2)}) async-start(bf16[8,128,2048]{2,0,1:T(8,128)(2,1)} %copy.21), calls=%async_computation.1 | async-start | bytes 8388608 | tf_op jit(solution)/shard_map/all_to_all | solution.py:67
  48.9 1.5 copy_bitcast_fusion.2
  50.4 3.1 %all_to_all.42 = f32[256,4,512]{2,0,1:T(8,128)} reshape(f32[32,8,4,4,128]{4,3,1,0,2:T(4,128)} %copy_bitcast_fusion.2) | data formatting | bytes 4194304 | tf_op jit(solution)/shard_map/all_to_all | solution.py:66
  53.9 43.2 %all-to-all-done.1 = bf16[8,128,2048]{2,0,1:T(8,128)(2,1)} async-done(((bf16[8,128,2048]{2,0,1:T(8,128)(2,1)}), bf16[8,128,2048]{2,0,1:T(8,128)(2,1)}, u32[]{:S(2)}, u32[]{:S(2)}) %all-to-all-start.1) | async-done | bytes 4194336 | tf_op jit(solution)/shard_map/all_to_all | solution.py:67
  97.2 3.2 %convert_reduce_fusion = f32[4,2048]{1,0:T(4,128)S(1)} fusion(bf16[32,8,4,2048]{3,1,2,0:T(8,128)(2,1)} %bitcast.20), kind=kLoop, calls=%fused_computation.60 | loop fusion | flops 4186112 | bytes 4227072 | tf_op jit(solution)/shard_map/reduce_sum | solution.py:72
  100.5 2.5 %copy_bitcast_fusion = bf16[256,4,2048]{2,0,1:T(8,128)(2,1)S(1)} fusion(bf16[8,128,2048]{2,0,1:T(8,128)(2,1)} %all-to-all-done.1), kind=kLoop, calls=%fused_computation.61 | loop fusion | bytes 8388608 | tf_op jit(solution)/shard_map/all_to_all | solution.py:67
  103.0 1.6 slice_bitcast_fusion.3
  104.8 2.3 while.58
  107.2 11.6 %while.59 = (s32[]{:T(128)}, f32[256,256]{1,0:T(8,128)S(1)}, f32[256]{0:T(256)S(1)}, s32[]{:T(128)}, f32[2048]{0:T(1024)S(1)}, /*index=5*/bf16[256,2048]{1,0:T(8...) while((s32[]{:T(128)}, f32[256,256]{1,0:T(8,128)S(1)}, ...), condition=%wide.region_5.6_spmd, body=%wide.region_4.5_spmd.sunk | while | flops 17170692 | bytes 665263 | solution.py:56
  109.6 1.1 convolution_add_fusion.10
  112.0 1.1 convolution_add_fusion.10
  118.8 6.3 %while.60 = (s32[]{:T(128)}, f32[256,256]{1,0:T(8,128)S(1)}, f32[256]{0:T(256)S(1)}, s32[]{:T(128)}, f32[2048]{0:T(1024)S(1)}, /*index=5*/bf16[256,2048]{1,0:T(8...) while((s32[]{:T(128)}, f32[256,256]{1,0:T(8,128)S(1)}, ...), condition=%wide.region_7.8_spmd, body=%wide.region_6.7_spmd.sunk | while | flops 17170692 | bytes 665263 | solution.py:56
  125.5 30.5 %while.62 = (s32[]{:T(128)}, bf16[4,256,256]{2,1,0:T(8,128)(2,1)}, f32[4,256,256]{2,1,0:T(8,128)S(1)}, f32[4,256]{1,0:T(4,128)S(1)}, s32[]{:T(128)}, /*index=5*/f32[]{:T(128)}) while((s32[]{:T(128)}, bf16[4,256,256]{2,1,0:T(8,128)(2,1)}, f32[4,256,256]{2,1,0:T(8,128)S(1)}, f32[4,256]{1,0:T(4,128)S(1)}, s32[]{:T(128)}, ...), condition=%wide.region_15.16_spmd, body=%wide.region_10.15_spmd.sunk | while | flops 2822701312 | bytes 12459699 | solution.py:95
  126.8 7.5 %conditional.2 = (bf16[1,256,256]{2,1,0:T(8,128)(2,1)S(1)}) conditional(s32[]{:T(128)} %convert_element_type.119, () %tuple.106, (f32[256,256]{1,0:T(8,128)S(1)}, f32[4,256]{1,0:T(4,128)S(1)}, s32[]{:T(128)}) %tuple.107), branch_computations={%region_12.12_spmd, %region_13.14_spmd} | conditional | flops 2822504704 | bytes 11672640 | solution.py:32
  136.3 7.5 %conditional.2 = (bf16[1,256,256]{2,1,0:T(8,128)(2,1)S(1)}) conditional(s32[]{:T(128)} %convert_element_type.119, () %tuple.106, (f32[256,256]{1,0:T(8,128)S(1)}, f32[4,256]{1,0:T(4,128)S(1)}, s32[]{:T(128)}) %tuple.107), branch_computations={%region_12.12_spmd, %region_13.14_spmd} | conditional | flops 2822504704 | bytes 11672640 | solution.py:32
  145.8 7.5 %conditional.2 = (bf16[1,256,256]{2,1,0:T(8,128)(2,1)S(1)}) conditional(s32[]{:T(128)} %convert_element_type.119, () %tuple.106, (f32[256,256]{1,0:T(8,128)S(1)}, f32[4,256]{1,0:T(4,128)S(1)}, s32[]{:T(128)}) %tuple.107), branch_computations={%region_12.12_spmd, %region_13.14_spmd} | conditional | flops 2822504704 | bytes 11672640 | solution.py:32
  156.0 3.0 %convolution_add_fusion.4 = f32[4,512,256]{2,1,0:T(8,128)} fusion(bf16[4,256,256]{2,1,0:T(8,128)(2,1)} %get-tuple-element.233, f32[256,4,512]{2,0,1:T(8,128)S(1)} %copy-done, f32[4,512]{1,0:T(4,128)S(1)} %bitcast.144), kind=kOutput, calls=%fused_computation.65 | convolution fusion | flops 270008320 | bytes 4726784 | tf_op jit(solution)/shard_map/tjk,jtf->ktf/dot_general | solution.py:96
  159.0 2.5 copy.24
  161.5 84.7 %all_to_all.54 = f32[256,4,4,128]{3,2,1,0:T(4,128)S(1)} all-to-all(f32[256,4,4,128]{3,2,1,0:T(4,128)S(1)} %copy.24), channel_id=1, replica_groups=mesh['ens'=32,'bal'=8] {'ens'}, dimensions={0} | all-to-all | bytes 4194304 | tf_op jit(solution)/shard_map/all_to_all | solution.py:100
  247.2 1.9 copy.27
  (178 shorter events, 46.2 us)
Async XLA Ops:
  3.5 36.1 %all-to-all-start = ((f32[8,128,4,128]{3,2,0,1:T(4,128)}), f32[8,128,4,128]{3,2,0,1:T(4,128)S(1)}, u32[]{:S(2)}, u32[]{:S(2)}) async-start(f32[8,128,4,128]{3,2,0,1:T(4,128)} %copy.19), calls=%async_computation | async-start | bytes 4194304 | tf_op jit(solution)/shard_map/all_to_all | solution.py:66
  39.6 57.6 %all-to-all-start.1 = ((bf16[8,128,2048]{2,0,1:T(8,128)(2,1)}), bf16[8,128,2048]{2,0,1:T(8,128)(2,1)}, u32[]{:S(2)}, u32[]{:S(2)}) async-start(bf16[8,128,2048]{2,0,1:T(8,128)(2,1)} %copy.21), calls=%async_computation.1 | async-start | bytes 8388608 | tf_op jit(solution)/shard_map/all_to_all | solution.py:67
  97.2 3.2 %copy-start.1 = (f32[4,2048]{1,0:T(4,128)S(1)}, f32[4,2048]{1,0:T(4,128)}, u32[]{:S(2)}) copy-start(f32[4,2048]{1,0:T(4,128)} %param.20) | copy-start | bytes 98308
  97.2 3.2 %copy-start.2 = (f32[4,2048]{1,0:T(4,128)S(1)}, f32[4,2048]{1,0:T(4,128)}, u32[]{:S(2)}) copy-start(f32[4,2048]{1,0:T(4,128)} %param.21) | copy-start | bytes 98308
  125.5 30.5 %copy-start = (f32[256,4,512]{2,0,1:T(8,128)S(1)}, f32[256,4,512]{2,0,1:T(8,128)}, u32[]{:S(2)}) copy-start(f32[256,4,512]{2,0,1:T(8,128)} %all_to_all.42) | copy-start | bytes 6291460
where the time goes:
time: 253 us; the launch traced here: 249 us
  blocking collectives  84.7 us (33%)
  waiting for transfers between devices  65.1 us (26%)
  matrix products  37.6 us (15%)
  local copies, waits for them, and re-layouts  30.8 us (12%)
  starting transfers between devices  13.1 us (5%)
  other arithmetic  9.01 us (4%)
  loops' own time  5.94 us (2%)
  between operations  2.79 us (1%)
    all_to_all x1, blocking collectives, body(): lax.all_to_all(result, 'ens', split_axis=0, concat_axis=1, tiled=True)  84.7 us
    all_to_all x1, waiting for transfers between devices, body(): lax.all_to_all(obs_ens, 'ens', split_axis=1, concat_axis=0, tiled=True)  43.2 us
    all_to_all x1, waiting for transfers between devices, body(): lax.all_to_all(members, 'ens', split_axis=1, concat_axis=0, tiled=True)  21.8 us
    unnamed x9, local copies, waits for them, and re-layouts  9.98 us
    dot_general x17, matrix products, add_block(): lax.dot_general(root_piece, root_piece, (((1,), (1,)), ((), ())), preferr...  9.12 us
    dot_general x17, matrix products, add_block(): jnp.dot(root_piece, rhs_piece, preferred_element_type=jnp.float32)  8.16 us
    all_to_all x1, starting transfers between devices, body(): lax.all_to_all(members, 'ens', split_axis=1, concat_axis=0, tiled=True)  7.76 us
    dot_general x15, matrix products, solve_weights(): jnp.dot(z_matrix, y_matrix, precision=highest)  5.57 us
  transfers between devices with their start and end apart: 2, of which 2 were waited for; matrix products, arithmetic and copies ran while one was open for 4% of the time, Pallas kernels for 0%

commit v1 on v0

--- a/solution.py
+++ b/solution.py
@@ -1,9 +1,23 @@
+import functools
+
 import jax
 import jax.numpy as jnp
 from jax import lax
+from jax.experimental import pallas as pl
+from jax.experimental.pallas import tpu as pltpu
 from jax.sharding import PartitionSpec as P
 
 NEWTON = 5
+MESH = pl.DeviceIdType.MESH
+WAYS = 32
+GROUP = 128
+LANES = 128
+SLOT_BLOCKS = 16
+HELD = 3
+CAPACITY = 24
+ROWS = 8
+ENS = 256
+CODE = 32767.0 / 6.0
 
 
 def solve_weights(gram_matrix, obs_vector):
@@ -56,7 +70,7 @@
     return lax.fori_loop(0, block_count, add_block, zero_sums)
 
 
-def body(members, obs_ens, obs_count, obs_value, obs_weight):
+def static_body(members, obs_ens, obs_count, obs_value, obs_weight):
     member_block, tile_block, nfield, columns = members.shape
     ens_ways = lax.axis_size("ens")
     ens_size = member_block * ens_ways
@@ -100,6 +114,367 @@
     return lax.all_to_all(result, "ens", split_axis=0, concat_axis=1, tiled=True)
 
 
+def ranks_of(sizes):
+    width = sizes.shape[-1]
+    here, there = sizes[..., :, None], sizes[..., None, :]
+    at = lax.broadcasted_iota(jnp.int32, (width, width), 0)
+    other = lax.broadcasted_iota(jnp.int32, (width, width), 1)
+    ahead = (there > here) | ((there == here) & (other < at))
+    return jnp.sum(ahead.astype(jnp.int32), axis=-1)
+
+
+def by_rank(ranks, values):
+    width = ranks.shape[-1]
+    place = lax.broadcasted_iota(jnp.int32, (width, width), 0)
+    hit = ranks[..., None, :] == place
+    return jnp.sum(jnp.where(hit, values[..., None, :], 0), axis=-1)
+
+
+def make_plan(obs_count):
+    counts = obs_count.reshape(-1, GROUP)
+    blocks = (counts + LANES - 1) // LANES
+    ranks = ranks_of(blocks)
+    ordered = by_rank(ranks, blocks)
+    tile_ids = jnp.broadcast_to(lax.iota(jnp.int32, GROUP), counts.shape)
+    ordered_tile = by_rank(ranks, tile_ids)
+    ordered_count = by_rank(ranks, counts)
+    first, second = ordered[:, :WAYS], ordered[:, 2 * WAYS - 1 : WAYS - 1 : -1]
+    pair_rank = ranks_of(first + second)
+    reverse = slice(3 * WAYS - 1, 2 * WAYS - 1, -1)
+    hit = pair_rank[..., :, None] == lax.iota(jnp.int32, WAYS)[None, None, :]
+
+    def third_of(array):
+        return jnp.sum(jnp.where(hit, array[:, None, reverse], 0), axis=-1)
+
+    third = third_of(ordered)
+    load = first + second + third
+    fits = (jnp.max(load) <= CAPACITY) & (jnp.max(ordered[:, HELD * WAYS]) == 0)
+    mine = lax.axis_index("bal")
+
+    def pick(array):
+        return lax.dynamic_index_in_dim(array, mine, 0, keepdims=False)
+
+    def three(array):
+        return jnp.stack(
+            [array[:, :WAYS], array[:, 2 * WAYS - 1 : WAYS - 1 : -1], third_of(array)], axis=-1
+        )
+
+    tiles = pick(three(ordered_tile))
+    tile_counts = pick(three(ordered_count))
+    tile_blocks = pick(jnp.stack([first, second, third], axis=-1))
+    place = lax.broadcasted_iota(jnp.int32, (WAYS, CAPACITY), 1)
+    one, two = tile_blocks[:, 0:1], tile_blocks[:, 0:1] + tile_blocks[:, 1:2]
+    end = two + tile_blocks[:, 2:3]
+    which = (place >= one).astype(jnp.int32) + (place >= two).astype(jnp.int32)
+
+    def chosen(array):
+        return jnp.where(which == 0, array[:, 0:1], jnp.where(which == 1, array[:, 1:2], array[:, 2:3]))
+
+    live = place < end
+    at_block = place - jnp.where(which == 0, 0, jnp.where(which == 1, one, two))
+    at_block = jnp.where(live, at_block, 0)
+    at_tile = chosen(tiles)
+    at_count = jnp.where(live, chosen(tile_counts) - at_block * LANES, 0)
+    source = at_block * GROUP + at_tile
+    weight_row = at_tile * SLOT_BLOCKS + at_block
+    return fits, tiles, tile_blocks, source, weight_row, at_count, which
+
+
+def pack_kernel(source, tiles, obs_hbm, members, obs_out, mem_out, obs_in, wide, sems):
+    pairs = CAPACITY // 2
+    copies = [
+        pltpu.make_async_copy(obs_hbm.at[m], obs_in.at[m], sems.at[m]) for m in range(ROWS)
+    ]
+    for copy in copies:
+        copy.start()
+
+    def pack_members(dest, carry):
+        for slot in range(HELD):
+            row = tiles[dest * HELD + slot] * 4
+            parts = [members[pl.ds(row + f, ROWS, stride=4 * GROUP), :] for f in range(4)]
+            coded = jnp.round(jnp.concatenate(parts, axis=0) * CODE)
+            mem_out[dest, slot] = coded.astype(jnp.int32).astype(jnp.int16)
+        return carry
+
+    lax.fori_loop(0, WAYS, pack_members, 0)
+
+    for m in range(ROWS):
+        copies[m].wait()
+
+        def widen(block, carry):
+            first = pl.multiple_of((m * SLOT_BLOCKS + block) * GROUP, GROUP)
+            lanes = pl.ds(pl.multiple_of(block * LANES, LANES), LANES)
+            wide[pl.ds(first, GROUP), :] = obs_in[m, :, lanes].astype(jnp.float32)
+            return carry
+
+        lax.fori_loop(0, SLOT_BLOCKS, widen, 0)
+
+    stride = SLOT_BLOCKS * GROUP
+
+    def pack_obs(dest, carry):
+        for pair in range(pairs):
+            at = dest * CAPACITY + 2 * pair
+            top = wide[pl.ds(source[at], ROWS, stride=stride), :]
+            low = wide[pl.ds(source[at + 1], ROWS, stride=stride), :]
+            obs_out[dest, pair] = jnp.concatenate([top, low], axis=0).astype(jnp.bfloat16)
+        return carry
+
+    lax.fori_loop(0, WAYS, pack_obs, 0)
+
+
+def pack(source, tiles, obs_ens, members):
+    smem = pl.BlockSpec(memory_space=pltpu.SMEM)
+    vmem = pl.BlockSpec(memory_space=pltpu.VMEM)
+    return pl.pallas_call(
+        pack_kernel,
+        out_shape=(
+            jax.ShapeDtypeStruct((WAYS, CAPACITY // 2, 16, LANES), jnp.bfloat16),
+            jax.ShapeDtypeStruct((WAYS, HELD, 32, LANES), jnp.int16),
+        ),
+        in_specs=[smem, smem, pl.BlockSpec(memory_space=pl.ANY), vmem],
+        out_specs=(vmem, vmem),
+        scratch_shapes=[
+            pltpu.VMEM((ROWS, GROUP, SLOT_BLOCKS * LANES), jnp.bfloat16),
+            pltpu.VMEM((ROWS * SLOT_BLOCKS * GROUP, LANES), jnp.float32),
+            pltpu.SemaphoreType.DMA((ROWS,)),
+        ],
+        compiler_params=pltpu.CompilerParams(vmem_limit_bytes=40 << 20),
+        name="pack",
+    )(source.reshape(-1), tiles.reshape(-1), obs_ens, members)
+
+
+def displacements():
+    every = [(dx, dy, dc) for dx in range(4) for dy in range(4) for dc in range(2)][1:]
+    return sorted(every, key=lambda d: -(min(d[0], 4 - d[0]) + min(d[1], 4 - d[1])))
+
+
+def shifted(me, step):
+    x, y, core = me // 8, (me // 2) % 4, me % 2
+    return (((x + step[0]) % 4) * 4 + (y + step[1]) % 4) * 2 + (core + step[2]) % 2
+
+
+def split(c, matrix, eye):
+    mean = jnp.sum(matrix * eye) * (1.0 / ENS)
+    deviation = matrix - mean * eye
+    return c + mean, deviation, deviation.astype(jnp.bfloat16)
+
+
+def times(left, right, eye):
+    cross = left[0] * right[1] + right[0] * left[1]
+    inner = jnp.dot(left[2], right[2], preferred_element_type=jnp.float32)
+    return split(left[0] * right[0], cross + inner, eye)
+
+
+def middle_of(product):
+    return 1.5 - 0.5 * product[0], -0.5 * product[1], product[2] * jnp.bfloat16(-0.5)
+
+
+def row_times(row, z):
+    high = row.astype(jnp.bfloat16)
+    low = (row - high.astype(jnp.float32)).astype(jnp.bfloat16)
+    rest = (z[1] - z[2].astype(jnp.float32)).astype(jnp.bfloat16)
+    out = jnp.dot(high, z[2], preferred_element_type=jnp.float32)
+    out = out + jnp.dot(low, z[2], preferred_element_type=jnp.float32)
+    out = out + jnp.dot(high, rest, preferred_element_type=jnp.float32)
+    return z[0] * row + out
+
+
+def analyse_kernel(
+    weight_row, at_count, which,
+    obs_send, mem_send, weights, values,
+    out_recv,
+    obs_recv, mem_recv, out_send, root, sel,
+    obs_ssem, obs_rsem, mem_ssem, mem_rsem, out_ssem, out_rsem, own_sem,
+):
+    me = lax.axis_index("ens")
+    steps = displacements()
+    targets = [shifted(me, step) for step in steps]
+    barrier = pltpu.get_barrier_semaphore()
+    for target in targets:
+        pl.semaphore_signal(barrier, inc=1, device_id={"ens": target}, device_id_type=MESH)
+    pl.semaphore_wait(barrier, WAYS - 1)
+
+    def exchange(src, dst, ssem, rsem, own):
+        copies = [
+            pltpu.make_async_remote_copy(
+                src_ref=src.at[target],
+                dst_ref=dst.at[me],
+                send_sem=ssem.at[i],
+                recv_sem=rsem.at[i],
+                device_id={"ens": target},
+                device_id_type=MESH,
+            )
+            for i, target in enumerate(targets)
+        ]
+        for copy in copies:
+            copy.start()
+        copies.append(pltpu.make_async_copy(src.at[me], dst.at[me], own))
+        copies[-1].start()
+        return copies
+
+    obs_copies = exchange(obs_send, obs_recv, obs_ssem, obs_rsem, own_sem.at[0])
+    mem_copies = exchange(mem_send, mem_recv, mem_ssem, mem_rsem, own_sem.at[1])
+    for copy in obs_copies:
+        copy.wait()
+
+    lane = lax.broadcasted_iota(jnp.int32, (1, LANES), 1)
+    for block in range(CAPACITY):
+        half = (block % 2) * ROWS
+        columns = pl.ds(block * LANES, LANES)
+        seen = obs_recv[:, block // 2].astype(jnp.float32)[:, half : half + ROWS, :]
+        seen = seen.reshape(ENS, LANES)
+        mean = jnp.sum(seen, axis=0, keepdims=True) * (1.0 / ENS)
+        at = me * CAPACITY + block
+        live = lane < at_count[at]
+        scale = jnp.where(live, jnp.sqrt(weights[pl.ds(weight_row[at], 1), :]), 0.0)
+        innov = scale * (values[pl.ds(weight_row[at], 1), :] - mean)
+        root[0:ENS, columns] = (scale * (seen - mean)).astype(jnp.bfloat16)
+        root[ENS : ENS + 16, columns] = jnp.broadcast_to(innov, (16, LANES)).astype(jnp.bfloat16)
+        for slot in range(HELD):
+            mine = (which[at] == slot).astype(jnp.float32)
+            sel[slot, :, columns] = jnp.full((16, LANES), mine, jnp.float32).astype(jnp.bfloat16)
+
+    rows = lax.broadcasted_iota(jnp.int32, (ENS, ENS), 0)
+    cols = lax.broadcasted_iota(jnp.int32, (ENS, ENS), 1)
+    eye = (rows == cols).astype(jnp.float32)
+    weight_t = []
+    for slot in range(HELD):
+        part = root[0:ENS, :] * sel[slot, 0:1, :]
+        sums = lax.dot_general(
+            root[...], part, (((1,), (1,)), ((), ())), preferred_element_type=jnp.float32
+        )
+        gram, vec = sums[0:ENS], sums[ENS : ENS + 8]
+        bound = (ENS - 1.0) + jnp.sum(gram * eye)
+        y = split((ENS - 1.0) / bound, gram * (1.0 / bound), eye)
+        middle = middle_of(y)
+        z = middle
+        y = times(y, middle, eye)
+        for iteration in range(1, NEWTON):
+            middle = middle_of(times(z, y, eye))
+            if iteration < NEWTON - 1:
+                y = times(y, middle, eye)
+            z = times(middle, z, eye)
+        shift = row_times(row_times(vec, z), z)[0:1] * (1.0 / bound)
+        factor = jnp.sqrt(jnp.float32(ENS - 1.0)) / jnp.sqrt(bound)
+        weight_t.append((factor * z[1] + (factor * z[0]) * eye + shift).astype(jnp.bfloat16))
+
+    for copy in mem_copies:
+        copy.wait()
+    out_copies = []
+    for slot in range(HELD):
+        coded = mem_recv[:, slot].astype(jnp.int32).astype(jnp.float32)
+        fields = [coded[:, f * ROWS : (f + 1) * ROWS, :].reshape(ENS, LANES) for f in range(4)]
+        state = jnp.concatenate(fields, axis=1) * (1.0 / CODE)
+        mean = jnp.sum(state, axis=0, keepdims=True) * (1.0 / ENS)
+        pert = (state - mean).astype(jnp.bfloat16)
+        result = mean + jnp.dot(weight_t[slot], pert, preferred_element_type=jnp.float32)
+        parts = [
+            result[:, f * LANES : (f + 1) * LANES].reshape(WAYS, ROWS, LANES) for f in range(4)
+        ]
+        out_send[slot] = jnp.concatenate(parts, axis=1).astype(jnp.bfloat16)
+        for i, target in enumerate(targets):
+            copy = pltpu.make_async_remote_copy(
+                src_ref=out_send.at[slot, target],
+                dst_ref=out_recv.at[slot, me],
+                send_sem=out_ssem.at[slot, i],
+                recv_sem=out_rsem.at[slot, i],
+                device_id={"ens": target},
+                device_id_type=MESH,
+            )
+            copy.start()
+            out_copies.append(copy)
+        copy = pltpu.make_async_copy(
+            out_send.at[slot, me], out_recv.at[slot, me], own_sem.at[2 + slot]
+        )
+        copy.start()
+        out_copies.append(copy)
+    for copy in out_copies:
+        copy.wait()
+
+
+def exchange_and_analyse(weight_row, at_count, which, obs_send, mem_send, weights, values):
+    smem = pl.BlockSpec(memory_space=pltpu.SMEM)
+    vmem = pl.BlockSpec(memory_space=pltpu.VMEM)
+    anywhere = pl.BlockSpec(memory_space=pl.ANY)
+    others = WAYS - 1
+    return pl.pallas_call(
+        analyse_kernel,
+        out_shape=jax.ShapeDtypeStruct((HELD, WAYS, 32, LANES), jnp.bfloat16),
+        in_specs=[smem, smem, smem, anywhere, anywhere, vmem, vmem],
+        out_specs=anywhere,
+        scratch_shapes=[
+            pltpu.VMEM((WAYS, CAPACITY // 2, 16, LANES), jnp.bfloat16),
+            pltpu.VMEM((WAYS, HELD, 32, LANES), jnp.int16),
+            pltpu.VMEM((HELD, WAYS, 32, LANES), jnp.bfloat16),
+            pltpu.VMEM((ENS + 16, CAPACITY * LANES), jnp.bfloat16),
+            pltpu.VMEM((HELD, 16, CAPACITY * LANES), jnp.bfloat16),
+            pltpu.SemaphoreType.DMA((others,)),
+            pltpu.SemaphoreType.DMA((others,)),
+            pltpu.SemaphoreType.DMA((others,)),
+            pltpu.SemaphoreType.DMA((others,)),
+            pltpu.SemaphoreType.DMA((HELD, others)),
+            pltpu.SemaphoreType.DMA((HELD, others)),
+            pltpu.SemaphoreType.DMA((2 + HELD,)),
+        ],
+        compiler_params=pltpu.CompilerParams(
+            collective_id=0, has_side_effects=True, vmem_limit_bytes=48 << 20
+        ),
+        name="analyse",
+    )(
+        weight_row.reshape(-1), at_count.reshape(-1), which.reshape(-1),
+        obs_send, mem_send, weights, values,
+    )
+
+
+def scatter_kernel(tiles, tile_blocks, members, recv, out):
+    out[...] = members[...]
+
+    def place(dest, carry):
+        for slot in range(HELD):
+            row = tiles[dest * HELD + slot] * 4
+
+            @pl.when(tile_blocks[dest * HELD + slot] > 0)
+            def _():
+                wide = recv[slot, dest].astype(jnp.float32)
+                for f in range(4):
+                    out[pl.ds(row + f, ROWS, stride=4 * GROUP), :] = wide[f * ROWS : (f + 1) * ROWS]
+
+        return carry
+
+    lax.fori_loop(0, WAYS, place, 0)
+
+
+def scatter(tiles, tile_blocks, members, recv):
+    smem = pl.BlockSpec(memory_space=pltpu.SMEM)
+    vmem = pl.BlockSpec(memory_space=pltpu.VMEM)
+    return pl.pallas_call(
+        scatter_kernel,
+        out_shape=jax.ShapeDtypeStruct(members.shape, jnp.float32),
+        in_specs=[smem, smem, vmem, vmem],
+        out_specs=vmem,
+        compiler_params=pltpu.CompilerParams(vmem_limit_bytes=40 << 20),
+        name="scatter",
+    )(tiles.reshape(-1), tile_blocks.reshape(-1), members, recv)
+
+
+def body(members, obs_ens, obs_count, obs_value, obs_weight):
+    fits, tiles, tile_blocks, source, weight_row, at_count, which = make_plan(obs_count)
+
+    def compact(members, obs_ens, obs_count, obs_value, obs_weight):
+        flat = members.reshape(-1, LANES)
+        weights = lax.all_gather(obs_weight, "ens", axis=0, tiled=True).reshape(-1, LANES)
+        values = lax.all_gather(obs_value, "ens", axis=0, tiled=True).reshape(-1, LANES)
+        obs_send, mem_send = pack(source, tiles, obs_ens, flat)
+        recv = exchange_and_analyse(
+            weight_row, at_count, which, obs_send, mem_send, weights, values
+        )
+        return scatter(tiles, tile_blocks, flat, recv).reshape(members.shape)
+
+    return lax.cond(
+        fits, compact, static_body, members, obs_ens, obs_count, obs_value, obs_weight
+    )
+
+
 def solution(mesh):
     in_specs = (
         P("ens", "bal", None, None),

time: 253 us -> 192 us (0.76)
  the two profiles are of different devices: /device:TPU:129 before, /device:TPU:1 now
where the time goes in v1:
time: 192 us
  waiting for transfers between devices  89.6 us (47%)
  Pallas kernels  67.5 us (35%)
  between operations  14.7 us (8%)
  local copies, waits for them, and re-layouts  11.3 us (6%)
  other arithmetic  8.01 us (4%)
    pallas_call x1, Pallas kernels, exchange_and_analyse(): pl.pallas_call(analyse_kernel, out_shape=jax.ShapeDtypeStruct((HELD, WAYS...  55.8 us
    all_gather x1, waiting for transfers between devices, compact(): lax.all_gather(obs_value, 'ens', axis=0, tiled=True).reshape(-1, LANES)  48 us
    all_gather x1, waiting for transfers between devices, compact(): lax.all_gather(obs_weight, 'ens', axis=0, tiled=True).reshape(-1, LANES)  40.3 us
    pallas_call x1, Pallas kernels, pack(): pl.pallas_call(pack_kernel, out_shape=(jax.ShapeDtypeStruct((WAYS, CAPACI...  8.17 us
  transfers between devices with their start and end apart: 2, of which 2 were waited for; matrix products, arithmetic and copies ran while one was open for 3% of the time, Pallas kernels for 4%

profile of v1, /device:TPU:1, one launch (start us, length us, event | category | flops | bytes accessed | tf_op | source)
XLA Modules:
  0.0 191.6 jit_solution(1579826910690784052)
XLA Ops:
  6.5 0.7 add_select_fusion
  7.6 1.2 select_reduce_fusion.2
  10.9 0.7 subtract_select_fusion
  11.5 0.7 fusion.44
  12.2 0.7 iota_compare_fusion.9
  14.1 0.6 add_reduce_fusion
  15.4 0.7 slice_reduce_fusion.4
  16.8 168.0 %conditional.2 = (f32[8,128,4,128]{3,2,1,0:T(4,128)}) conditional(s32[]{:T(128)} %convert_element_type.68, (f32[8,128,4,128]{3,2,1,0:T(4,128)}, s32[1024]{0:T(1024)}, bf16[8,128,2048]{2,1,0:T(8,128)(2,1)}, f32[4,2048]{1,0:T(4,128)}, f32[4,2048]{1,0:T(4,128)}) %tuple.41, (s32[32,3]{0,1:T(4,128)S(1)}, s32[32,3]{0,1:T(4,128)}, ...), branch_computations={%region_10.27_spmd, %region_27.28_spmd} | conditional | flops 3166949632 | bytes 115961680 | solution.py:473
  17.1 0.7 all-gather.5.cloned.1.call-update
  17.8 0.7 all-gather.7.cloned.1.call-update
  18.5 0.7 constant_dynamic-slice_fusion
  19.3 0.9 fusion.36
  20.3 0.8 copy.68
  21.3 0.8 reshape.137.which
  22.1 0.7 copy.69
  22.9 8.2 %pack.1 = (bf16[32,12,16,128]{3,2,1,0:T(8,128)(2,1)S(1)}, s16[32,3,32,128]{3,2,1,0:T(8,128)(2,1)S(1)}) custom-call(s32[768]{0:T(1024)S(1)} %reshape.138.source, s32[96]{0:T(128)S(1)} %reshape.132.tiles, bf16[8,128,2048]{2,1,0:T(8,128)(2,1)} %get-tuple-element.270.obs_hbm, f32[4096,128]{1,0:T(8,128)} %bitcast.177), custom_call_target="tpu_custom_call" | custom-call | tf_op jit(solution)/shard_map/cond/branch_1_fun/pack/pallas_call | solution.py:228
  31.1 1.1 copy-done
  32.2 40.3 %all-gather.5.cloned.1.call-done = f32[32,4,2048]{2,1,0:T(4,128)} async-done(((f32[1,4,2048]{2,1,0:T(4,128)}), f32[32,4,2048]{2,1,0:T(4,128)}) %all-gather.5.cloned.1.call-update) | async-done | bytes 1048592 | tf_op jit(solution)/shard_map/cond/branch_1_fun/all_gather | solution.py:465
  72.5 1.8 reshape.139.weights
  74.3 48.0 %all-gather.7.cloned.1.call-done = f32[32,4,2048]{2,1,0:T(4,128)} async-done(((f32[1,4,2048]{2,1,0:T(4,128)}), f32[32,4,2048]{2,1,0:T(4,128)}) %all-gather.7.cloned.1.call-update) | async-done | bytes 1048592 | tf_op jit(solution)/shard_map/cond/branch_1_fun/all_gather | solution.py:466
  122.3 1.8 reshape.140.values
  124.0 1.4 copy-done.1
  125.4 55.8 %analyse.1.recv = bf16[3,32,32,128]{3,2,1,0:T(8,128)(2,1)S(1)} custom-call(s32[768]{0:T(1024)S(1)} %reshape.135.weight_row, s32[768]{0:T(1024)S(1)} %reshape.136.at_count, s32[768]{0:T(1024)S(1)} %reshape.137.which, bf16[32,12,16,128]{3,2,1,0:T(8,128)(2,1)S(1)} %copy-done.1, s16[32,3,32,128]{3,2,1,0:T(8,128)(2,1)S(1)} %get-tuple-element.272.mem_send, ...), custom_call_target="tpu_custom_call" | custom-call | tf_op jit(solution)/shard_map/cond/branch_1_fun/analyse/pallas_call | solution.py:400
  181.2 3.5 %scatter.1 = f32[4096,128]{1,0:T(8,128)} custom-call(s32[96]{0:T(128)S(1)} %reshape.132.tiles, s32[96]{0:T(128)S(1)} %reshape.133.tile_blocks, f32[4096,128]{1,0:T(8,128)S(1)} %bitcast.178, bf16[3,32,32,128]{3,2,1,0:T(8,128)(2,1)S(1)} %analyse.1.recv), custom_call_target="tpu_custom_call" | custom-call | tf_op jit(solution)/shard_map/cond/branch_1_fun/scatter/pallas_call | solution.py:450
  (39 shorter events, 4.2 us)
Async XLA Ops:
  10.8 2.0 %copy-start.6 = (s32[1,32,3]{1,2,0:T(4,128)}, s32[1,32,3]{1,2,0:T(4,128)S(1)}, u32[]{:S(2)}) copy-start(s32[1,32,3]{1,2,0:T(4,128)S(1)} %copy.91) | copy-start | bytes 1156
  17.0 3.1 %copy-start.7 = (s32[32,3]{0,1:T(4,128)}, s32[32,3]{0,1:T(4,128)S(1)}, u32[]{:S(2)}) copy-start(s32[32,3]{0,1:T(4,128)S(1)} %get-tuple-element.396) | copy-start | bytes 1156 | tf_op jit(solution)/shard_map/cond
  17.0 55.5 %all-gather.5.cloned.1.call-start = ((), (), s32[]{:S(2)}) async-start(), calls=%async_computation.3 | async-start | bytes 1081344 | tf_op jit(solution)/shard_map/cond/branch_1_fun/all_gather | solution.py:465
  17.8 104.5 %all-gather.7.cloned.1.call-start = ((), (), s32[]{:S(2)}) async-start(), calls=%async_computation.4 | async-start | bytes 1081344 | tf_op jit(solution)/shard_map/cond/branch_1_fun/all_gather | solution.py:466
  31.1 1.1 copy-start
  124.0 1.4 copy-start.1
  125.4 55.8 %copy-start.2 = (f32[8,128,4,128]{3,2,1,0:T(4,128)S(1)}, f32[8,128,4,128]{3,2,1,0:T(4,128)}, u32[]{:S(2)}) copy-start(f32[8,128,4,128]{3,2,1,0:T(4,128)} %get-tuple-element.265) | copy-start | bytes 6291460 | tf_op jit(solution)/shard_map/cond
Sparse Core Ops, SparseCore 0:
  20.4 52.0 all-gather.4
  75.1 47.1 all-gather.6

commit v2 on v0

--- a/solution.py
+++ b/solution.py
@@ -1,9 +1,27 @@
+import functools
+
 import jax
 import jax.numpy as jnp
 from jax import lax
+from jax.experimental import pallas as pl
+from jax.experimental.pallas import tpu as pltpu
 from jax.sharding import PartitionSpec as P
 
 NEWTON = 5
+MESH = pl.DeviceIdType.MESH
+WAYS = 32
+GROUP = 128
+LANES = 128
+SLOT_BLOCKS = 16
+HELD = 3
+CAPACITY = 24
+THIRD = 4
+ROWS = 8
+ENS = 256
+CODE = 32767.0 / 6.0
+ROOT_CODE = 32767.0 / 0.708
+TILE_ROWS = 4 * SLOT_BLOCKS
+AT_TILE, AT_BLOCKS, AT_COUNT = 32, 36, 64
 
 
 def solve_weights(gram_matrix, obs_vector):
@@ -56,7 +74,7 @@
     return lax.fori_loop(0, block_count, add_block, zero_sums)
 
 
-def body(members, obs_ens, obs_count, obs_value, obs_weight):
+def static_body(members, obs_ens, obs_count, obs_value, obs_weight):
     member_block, tile_block, nfield, columns = members.shape
     ens_ways = lax.axis_size("ens")
     ens_size = member_block * ens_ways
@@ -100,6 +118,460 @@
     return lax.all_to_all(result, "ens", split_axis=0, concat_axis=1, tiled=True)
 
 
+def plan_kernel(counts, table, fits):
+    lane = lax.broadcasted_iota(jnp.int32, (8, LANES), 1)
+    device = lane % WAYS
+    tiles = counts[...]
+    key = tiles * GROUP + lane
+    rank = jnp.zeros_like(key)
+    for step in range(1, GROUP):
+        rank += (pltpu.roll(key, step, 1) > key).astype(jnp.int32)
+    first, second, third = jnp.zeros_like(key), jnp.zeros_like(key), jnp.zeros_like(key)
+    third_rank = jnp.where(device % 2 == 0, 79 - device // 2, -1)
+    for step in range(GROUP):
+        there = pltpu.roll(rank, step, 1) if step else rank
+        value = pltpu.roll(key, step, 1) if step else key
+        first = jnp.where(there == device, value, first)
+        second = jnp.where(there == 2 * WAYS - 1 - device, value, second)
+        third = jnp.where(there == third_rank, value, third)
+
+    def blocks_of(array):
+        return (array // GROUP + LANES - 1) // LANES
+
+    pair = (blocks_of(first) + blocks_of(second)) * WAYS + device
+    pair_rank = jnp.zeros_like(pair)
+    for step in range(1, WAYS):
+        pair_rank += (pltpu.roll(pair, step, 1) > pair).astype(jnp.int32)
+    wanted = device // 2 + jnp.where(device % 2 == 0, WAYS // 2, 0)
+    one, two = jnp.zeros_like(key), jnp.zeros_like(key)
+    for step in range(WAYS):
+        hit = (pltpu.roll(pair_rank, step, 1) if step else pair_rank) == wanted
+        one = jnp.where(hit, pltpu.roll(first, step, 1) if step else first, one)
+        two = jnp.where(hit, pltpu.roll(second, step, 1) if step else second, two)
+    load = blocks_of(one) + blocks_of(two) + blocks_of(third)
+    over = (load > CAPACITY) | (blocks_of(third) > THIRD) | ((rank >= 80) & (tiles > 0))
+    fits[0, 0] = 1 - jnp.max(over.astype(jnp.int32))
+
+    row = lax.broadcasted_iota(jnp.int32, (8, LANES), 0)
+    wide_lane = lax.broadcasted_iota(jnp.int32, (WAYS, LANES), 1)
+    wide_row = lax.broadcasted_iota(jnp.int32, (WAYS, LANES), 0)
+
+    def column(array):
+        mine = jnp.sum(jnp.where(row == lax.axis_index("bal"), array, 0), axis=0, keepdims=True)
+        mine = jnp.broadcast_to(mine, (WAYS, LANES))
+        return jnp.sum(jnp.where(wide_lane == wide_row, mine, 0), axis=1, keepdims=True)
+
+    keys = [column(array) for array in (one, two, third)]
+    size = [blocks_of(array) for array in keys]
+    start = [jnp.zeros_like(size[0]), CAPACITY - size[2] - size[1], CAPACITY - size[2]]
+
+    def table_of(place):
+        at_key, at_block = jnp.broadcast_to(keys[0], place.shape), jnp.full_like(place, -1)
+        for slot in range(HELD):
+            here = (place >= start[slot]) & (place < start[slot] + size[slot])
+            at_key = jnp.where(here, keys[slot], at_key)
+            at_block = jnp.where(here, place - start[slot], at_block)
+        return at_key, at_block
+
+    at_key, at_block = table_of(wide_lane)
+    out = jnp.maximum(at_block, 0) * GROUP + at_key % GROUP
+    at_key, at_block = table_of(wide_lane - AT_COUNT)
+    left = jnp.where(at_block >= 0, at_key // GROUP - at_block * LANES, 0)
+    out = jnp.where(wide_lane >= AT_COUNT, left, out)
+    for slot in range(HELD):
+        out = jnp.where(wide_lane == AT_TILE + slot, keys[slot] % GROUP, out)
+        out = jnp.where(wide_lane == AT_BLOCKS + slot, size[slot], out)
+    table[...] = out
+
+
+def make_plan(obs_count):
+    return pl.pallas_call(
+        plan_kernel,
+        out_shape=(
+            jax.ShapeDtypeStruct((WAYS, LANES), jnp.int32),
+            jax.ShapeDtypeStruct((1, 1), jnp.int32),
+        ),
+        in_specs=[pl.BlockSpec(memory_space=pltpu.VMEM)],
+        out_specs=(
+            pl.BlockSpec(memory_space=pltpu.VMEM),
+            pl.BlockSpec(memory_space=pltpu.SMEM),
+        ),
+        name="plan",
+    )(obs_count.reshape(8, GROUP))
+
+
+def displacements():
+    every = [(dx, dy, dc) for dx in range(4) for dy in range(4) for dc in range(2)][1:]
+    return sorted(every, key=lambda d: -(min(d[0], 4 - d[0]) + min(d[1], 4 - d[1])))
+
+
+def shifted(me, step, sign=1):
+    x, y, core = me // 8, (me // 2) % 4, me % 2
+    dx, dy = (step[0], step[1]) if sign > 0 else ((4 - step[0]) % 4, (4 - step[1]) % 4)
+    return (((x + dx) % 4) * 4 + (y + dy) % 4) * 2 + (core + step[2]) % 2
+
+
+def centred(c, matrix, eye):
+    half = ENS // 2
+    top, low = matrix[:half, :half], matrix[half:, half:]
+    mean = jnp.sum((top + low) * eye) * (1.0 / ENS)
+    upper = jnp.concatenate([top - mean * eye, matrix[:half, half:]], axis=1)
+    lower = jnp.concatenate([matrix[half:, :half], low - mean * eye], axis=1)
+    deviation = jnp.concatenate([upper, lower], axis=0)
+    return c + mean, deviation, deviation.astype(jnp.bfloat16)
+
+
+def times(left, right, eye):
+    cross = left[0] * right[1] + right[0] * left[1]
+    inner = jnp.dot(left[2], right[2], preferred_element_type=jnp.float32)
+    return centred(left[0] * right[0], cross + inner, eye)
+
+
+def middle_of(product):
+    return 1.5 - 0.5 * product[0], -0.5 * product[1], product[2] * jnp.bfloat16(-0.5)
+
+
+def row_times(row, z):
+    high = row.astype(jnp.bfloat16)
+    low = (row - high.astype(jnp.float32)).astype(jnp.bfloat16)
+    rest = (z[1] - z[2].astype(jnp.float32)).astype(jnp.bfloat16)
+    out = jnp.dot(high, z[2], preferred_element_type=jnp.float32)
+    out = out + jnp.dot(low, z[2], preferred_element_type=jnp.float32)
+    out = out + jnp.dot(high, rest, preferred_element_type=jnp.float32)
+    return z[0] * row + out
+
+
+def coded(array, scale):
+    return jnp.round(array * scale).astype(jnp.int32).astype(jnp.int16)
+
+
+def decoded(array, scale):
+    return array.astype(jnp.int32).astype(jnp.float32) * (1.0 / scale)
+
+
+def analyse_kernel(
+    table, obs_hbm, mem_hbm, values, weights,
+    out_recv,
+    obs_in, wide, mem_in, obs_send, mem_send, side_send, obs_recv, mem_recv, side_recv, side,
+    out_send, root, root_t,
+    in_sem, obs_ssem, obs_rsem, mem_ssem, mem_rsem, side_ssem, side_rsem, out_ssem, out_rsem, own_sem,
+):
+    me = lax.axis_index("ens")
+    core = me % 2
+    steps = displacements()
+    targets = [shifted(me, step) for step in steps]
+    sources = [shifted(me, step, -1) for step in steps]
+
+    def remote(src, dst, ssem, rsem, target):
+        return pltpu.make_async_remote_copy(
+            src_ref=src, dst_ref=dst, send_sem=ssem, recv_sem=rsem,
+            device_id={"ens": target}, device_id_type=MESH,
+        )
+
+    mem_load = pltpu.make_async_copy(mem_hbm, mem_in, in_sem.at[ROWS])
+    obs_loads = [
+        pltpu.make_async_copy(obs_hbm.at[m], obs_in.at[m], in_sem.at[m]) for m in range(ROWS)
+    ]
+    for copy in obs_loads:
+        copy.start()
+    mem_load.start()
+
+    barrier = pltpu.get_barrier_semaphore()
+    for target in targets:
+        pl.semaphore_signal(barrier, inc=1, device_id={"ens": target}, device_id_type=MESH)
+    side_send[0:TILE_ROWS] = coded(values[...], CODE)
+    side_send[TILE_ROWS : 2 * TILE_ROWS] = coded(jnp.sqrt(weights[...]), ROOT_CODE)
+    pl.semaphore_wait(barrier, WAYS - 1)
+
+    side_copies = []
+    for i, (step, target) in enumerate(zip(steps, targets)):
+        if step[2] == 0:
+            copy = remote(
+                side_send, side_recv.at[core, me // 2], side_ssem.at[i], side_rsem.at[i], target
+            )
+            copy.start()
+            side_copies.append(copy)
+    own_side = pltpu.make_async_copy(side_send, side_recv.at[core, me // 2], own_sem.at[0])
+    own_side.start()
+
+    for m in range(ROWS):
+        obs_loads[m].wait()
+
+        def widen(block, carry):
+            first = pl.multiple_of((m * SLOT_BLOCKS + block) * GROUP, GROUP)
+            lanes = pl.ds(pl.multiple_of(block * LANES, LANES), LANES)
+            wide[pl.ds(first, GROUP), :] = obs_in[m, :, lanes].astype(jnp.float32)
+            return carry
+
+        lax.fori_loop(0, SLOT_BLOCKS, widen, 0)
+
+    def pack_obs(dest):
+        for pair in range(CAPACITY // 2):
+            rows = [
+                wide[pl.ds(table[dest, 2 * pair + j], ROWS, stride=SLOT_BLOCKS * GROUP), :]
+                for j in range(2)
+            ]
+            obs_send[dest, pair] = jnp.concatenate(rows, axis=0).astype(jnp.bfloat16)
+
+    def pack_members(dest, slot):
+        row = table[dest, AT_TILE + slot] * 4
+        parts = [mem_in[pl.ds(row + f, ROWS, stride=4 * GROUP), :] for f in range(4)]
+        mem_send[slot, dest] = coded(jnp.concatenate(parts, axis=0), CODE)
+
+    obs_copies = []
+    for i, target in enumerate(targets):
+        pack_obs(target)
+        copy = remote(
+            obs_send.at[target], obs_recv.at[me], obs_ssem.at[i], obs_rsem.at[i], target
+        )
+        copy.start()
+        obs_copies.append(copy)
+    pack_obs(me)
+    copy = pltpu.make_async_copy(obs_send.at[me], obs_recv.at[me], own_sem.at[1])
+    copy.start()
+    obs_copies.append(copy)
+
+    mem_load.wait()
+    mem_copies = []
+    for slot in range(HELD):
+        for i, target in enumerate(targets):
+            pack_members(target, slot)
+            copy = remote(
+                mem_send.at[slot, target], mem_recv.at[slot, me],
+                mem_ssem.at[slot, i], mem_rsem.at[slot, i], target,
+            )
+            mem_copies.append(copy)
+            if slot < 2:
+                copy.start()
+            else:
+                pl.when(target % 2 == 0)(copy.start)
+        pack_members(me, slot)
+        copy = pltpu.make_async_copy(
+            mem_send.at[slot, me], mem_recv.at[slot, me], own_sem.at[2 + slot]
+        )
+        copy.start()
+        mem_copies.append(copy)
+
+    for copy in side_copies:
+        copy.wait()
+    own_side.wait()
+    partner = me + 1 - 2 * core
+    copy = remote(
+        side_recv.at[core], side_recv.at[core], side_ssem.at[WAYS - 1], side_rsem.at[WAYS - 1], partner
+    )
+    copy.start()
+    copy.wait()
+    for c in range(2):
+        for chip in range(WAYS // 2):
+            first = (chip * 2 + c) * 2 * TILE_ROWS
+            side[first : first + 2 * TILE_ROWS, :] = (
+                side_recv[c, chip].astype(jnp.int32).astype(jnp.float32)
+            )
+
+    for copy in obs_copies:
+        copy.wait()
+    lane = lax.broadcasted_iota(jnp.int32, (1, LANES), 1)
+    for block in range(CAPACITY):
+        half = (block % 2) * ROWS
+        columns = pl.ds(block * LANES, LANES)
+        seen = obs_recv[:, block // 2].astype(jnp.float32)[:, half : half + ROWS, :]
+        seen = seen.reshape(ENS, LANES)
+        mean = jnp.sum(seen, axis=0, keepdims=True) * (1.0 / ENS)
+        source = table[me, block]
+        tile, part = source % GROUP, source // GROUP
+        side_row = (tile // 4) * 2 * TILE_ROWS + (tile % 4) * SLOT_BLOCKS + part
+        live = lane < table[me, AT_COUNT + block]
+        scale = side[pl.ds(side_row + TILE_ROWS, 1), :] * (1.0 / ROOT_CODE)
+        scale = jnp.where(live, scale, 0.0)
+        innov = scale * (side[pl.ds(side_row, 1), :] * (1.0 / CODE) - mean)
+        rows = scale * (seen - mean)
+        root[0:ENS, columns] = rows.astype(jnp.bfloat16)
+        root[ENS : ENS + 16, columns] = jnp.broadcast_to(innov, (16, LANES)).astype(jnp.bfloat16)
+        root_t[block * LANES : (block + 1) * LANES, :] = rows.T.astype(jnp.bfloat16)
+
+    reach = [
+        (0, SLOT_BLOCKS),
+        ((CAPACITY - THIRD - CAPACITY // 2) // 2 * 2, CAPACITY),
+        (CAPACITY - THIRD, CAPACITY),
+    ]
+    size = [table[me, AT_BLOCKS + slot] for slot in range(HELD)]
+    start = [jnp.int32(0), CAPACITY - size[2] - size[1], CAPACITY - size[2]]
+    half = ENS // 2
+    eye = (
+        lax.broadcasted_iota(jnp.int32, (half, half), 0)
+        == lax.broadcasted_iota(jnp.int32, (half, half), 1)
+    ).astype(jnp.float32)
+    held = range(HELD)
+    vecs, bounds, ys = [], [], []
+    for slot in held:
+        low, high = reach[slot]
+        place = low + lax.broadcasted_iota(jnp.int32, (1, (high - low) * LANES), 1) // LANES
+        mine = (place >= start[slot]) & (place < start[slot] + size[slot])
+        part = root[:, low * LANES : high * LANES] * mine.astype(jnp.float32).astype(jnp.bfloat16)
+        sums = jnp.dot(
+            part, root_t[low * LANES : high * LANES, :], preferred_element_type=jnp.float32
+        )
+        gram = sums[0:ENS]
+        vecs.append(sums[ENS : ENS + 8])
+        trace = jnp.sum((gram[:half, :half] + gram[half:, half:]) * eye)
+        bound = (ENS - 1.0) + trace
+        bounds.append(bound)
+        ys.append(centred((ENS - 1.0) / bound, gram * (1.0 / bound), eye))
+    zs = middles = [middle_of(y) for y in ys]
+    ys = [times(ys[slot], middles[slot], eye) for slot in held]
+    for iteration in range(1, NEWTON):
+        middles = [middle_of(times(zs[slot], ys[slot], eye)) for slot in held]
+        if iteration < NEWTON - 1:
+            ys = [times(ys[slot], middles[slot], eye) for slot in held]
+        zs = [times(middles[slot], zs[slot], eye) for slot in held]
+    weight_t = []
+    for slot in held:
+        z, bound = zs[slot], bounds[slot]
+        shift = row_times(row_times(vecs[slot], z), z)[0:1] * (1.0 / bound)
+        factor = jnp.sqrt(jnp.float32(ENS - 1.0)) / jnp.sqrt(bound)
+        diagonal = (factor * z[0]) * eye
+        full = factor * z[1] + shift
+        upper = jnp.concatenate([full[:half, :half] + diagonal, full[:half, half:]], axis=1)
+        lower = jnp.concatenate([full[half:, :half], full[half:, half:] + diagonal], axis=1)
+        weight_t.append(jnp.concatenate([upper, lower], axis=0).astype(jnp.bfloat16))
+
+    others = WAYS - 1
+    out_copies = []
+    for slot in range(HELD):
+        for i in range(others):
+            copy = mem_copies[slot * WAYS + i]
+            if slot < 2:
+                copy.wait()
+            else:
+                pl.when(targets[i] % 2 == 0)(copy.wait_send)
+                pl.when(core == 0)(copy.wait_recv)
+        mem_copies[slot * WAYS + others].wait()
+        raw = decoded(mem_recv[slot], CODE)
+        fields = [raw[:, f * ROWS : (f + 1) * ROWS, :].reshape(ENS, LANES) for f in range(4)]
+        state = jnp.concatenate(fields, axis=1)
+        mean = jnp.sum(state, axis=0, keepdims=True) * (1.0 / ENS)
+        pert = (state - mean).astype(jnp.bfloat16)
+        result = mean + jnp.dot(weight_t[slot], pert, preferred_element_type=jnp.float32)
+        parts = [
+            result[:, f * LANES : (f + 1) * LANES].reshape(WAYS, ROWS, LANES) for f in range(4)
+        ]
+        out_send[slot] = jnp.concatenate(parts, axis=1).astype(jnp.bfloat16)
+        for i, target in enumerate(targets):
+            copy = remote(
+                out_send.at[slot, target], out_recv.at[slot, me],
+                out_ssem.at[slot, i], out_rsem.at[slot, i], target,
+            )
+            out_copies.append(copy)
+            if slot < 2:
+                copy.start()
+            else:
+                pl.when(core == 0)(copy.start)
+        copy = pltpu.make_async_copy(
+            out_send.at[slot, me], out_recv.at[slot, me], own_sem.at[2 + HELD + slot]
+        )
+        copy.start()
+        out_copies.append(copy)
+    for slot in range(HELD):
+        for i in range(others):
+            copy = out_copies[slot * WAYS + i]
+            if slot < 2:
+                copy.wait()
+            else:
+                pl.when(core == 0)(copy.wait_send)
+                pl.when(sources[i] % 2 == 0)(copy.wait_recv)
+        out_copies[slot * WAYS + others].wait()
+
+
+def exchange_and_analyse(table, obs_ens, members, values, weights):
+    smem = pl.BlockSpec(memory_space=pltpu.SMEM)
+    vmem = pl.BlockSpec(memory_space=pltpu.VMEM)
+    anywhere = pl.BlockSpec(memory_space=pl.ANY)
+    others = WAYS - 1
+    dma = pltpu.SemaphoreType.DMA
+    pairs = CAPACITY // 2
+    return pl.pallas_call(
+        analyse_kernel,
+        out_shape=jax.ShapeDtypeStruct((HELD, WAYS, 32, LANES), jnp.bfloat16),
+        in_specs=[smem, anywhere, anywhere, vmem, vmem],
+        out_specs=anywhere,
+        scratch_shapes=[
+            pltpu.VMEM((ROWS, GROUP, SLOT_BLOCKS * LANES), jnp.bfloat16),
+            pltpu.VMEM((ROWS * SLOT_BLOCKS * GROUP, LANES), jnp.float32),
+            pltpu.VMEM((ROWS * GROUP * 4, LANES), jnp.float32),
+            pltpu.VMEM((WAYS, pairs, 16, LANES), jnp.bfloat16),
+            pltpu.VMEM((HELD, WAYS, 32, LANES), jnp.int16),
+            pltpu.VMEM((2 * TILE_ROWS, LANES), jnp.int16),
+            pltpu.VMEM((WAYS, pairs, 16, LANES), jnp.bfloat16),
+            pltpu.VMEM((HELD, WAYS, 32, LANES), jnp.int16),
+            pltpu.VMEM((2, WAYS // 2, 2 * TILE_ROWS, LANES), jnp.int16),
+            pltpu.VMEM((WAYS * 2 * TILE_ROWS, LANES), jnp.float32),
+            pltpu.VMEM((HELD, WAYS, 32, LANES), jnp.bfloat16),
+            pltpu.VMEM((ENS + 16, CAPACITY * LANES), jnp.bfloat16),
+            pltpu.VMEM((CAPACITY * LANES, ENS), jnp.bfloat16),
+            dma((ROWS + 1,)),
+            dma((others,)),
+            dma((others,)),
+            dma((HELD, others)),
+            dma((HELD, others)),
+            dma((WAYS,)),
+            dma((WAYS,)),
+            dma((HELD, others)),
+            dma((HELD, others)),
+            dma((2 + 2 * HELD,)),
+        ],
+        compiler_params=pltpu.CompilerParams(
+            collective_id=0, has_side_effects=True, vmem_limit_bytes=56 << 20
+        ),
+        name="analyse",
+    )(table, obs_ens, members, values, weights)
+
+
+def scatter_kernel(table, members, recv, out):
+    out[...] = members[...]
+
+    def place(dest, carry):
+        for slot in range(HELD):
+            row = table[dest, AT_TILE + slot] * 4
+
+            @pl.when(table[dest, AT_BLOCKS + slot] > 0)
+            def _():
+                tall = recv[slot, dest].astype(jnp.float32)
+                for f in range(4):
+                    out[pl.ds(row + f, ROWS, stride=4 * GROUP), :] = tall[f * ROWS : (f + 1) * ROWS]
+
+        return carry
+
+    lax.fori_loop(0, WAYS, place, 0)
+
+
+def scatter(table, members, recv):
+    smem = pl.BlockSpec(memory_space=pltpu.SMEM)
+    vmem = pl.BlockSpec(memory_space=pltpu.VMEM)
+    return pl.pallas_call(
+        scatter_kernel,
+        out_shape=jax.ShapeDtypeStruct(members.shape, jnp.float32),
+        in_specs=[smem, vmem, vmem],
+        out_specs=vmem,
+        compiler_params=pltpu.CompilerParams(vmem_limit_bytes=40 << 20),
+        name="scatter",
+    )(table, members, recv)
+
+
+def body(members, obs_ens, obs_count, obs_value, obs_weight):
+    table, fits = make_plan(obs_count)
+
+    def compact(members, obs_ens, obs_count, obs_value, obs_weight):
+        flat = members.reshape(-1, LANES)
+        recv = exchange_and_analyse(
+            table, obs_ens, flat, obs_value.reshape(-1, LANES), obs_weight.reshape(-1, LANES)
+        )
+        return scatter(table, flat, recv).reshape(members.shape)
+
+    return lax.cond(
+        fits[0, 0] > 0, compact, static_body, members, obs_ens, obs_count, obs_value, obs_weight
+    )
+
+
 def solution(mesh):
     in_specs = (
         P("ens", "bal", None, None),

time: 253 us -> 66.9 us (0.26)
  the two profiles are of different devices: /device:TPU:129 before, /device:TPU:1 now
where the time goes in v2:
time: 66.9 us; the launch traced here: 66.6 us
  Pallas kernels  60.1 us (90%)
  local copies, waits for them, and re-layouts  5.23 us (8%)
  between operations  0.67 us (1%)
    pallas_call x1, Pallas kernels, exchange_and_analyse(): pl.pallas_call(analyse_kernel, out_shape=jax.ShapeDtypeStruct((HELD, WAYS...  55.4 us
    pallas_call x1, Pallas kernels, scatter(): pl.pallas_call(scatter_kernel, out_shape=jax.ShapeDtypeStruct(members.sha...  2.52 us
    pallas_call x1, Pallas kernels, make_plan(): pl.pallas_call(plan_kernel, out_shape=(jax.ShapeDtypeStruct((WAYS, LANES)...  2.17 us
    reshape x1, local copies, waits for them, and re-layouts, compact(): obs_value.reshape(-1, LANES)  1.39 us
    reshape x1, local copies, waits for them, and re-layouts, compact(): obs_weight.reshape(-1, LANES)  1.39 us

profile of v2, /device:TPU:1, one launch (start us, length us, event | category | flops | bytes accessed | tf_op | source)
XLA Modules:
  0.0 66.6 jit_solution(14426692677804170698)
XLA Ops:
  0.0 2.2 %plan.1 = (s32[32,128]{1,0:T(8,128)}, s32[1,1]{1,0:T(1,128)}) custom-call(s32[8,128]{1,0:T(8,128)} %bitcast.164), custom_call_target="tpu_custom_call" | custom-call | tf_op jit(solution)/shard_map/plan/pallas_call | solution.py:188
  2.8 62.4 %conditional.2 = (f32[8,128,4,128]{3,2,1,0:T(4,128)S(1)}) conditional(s32[]{:T(128)} %bitcast.53, (f32[8,128,4,128]{3,2,1,0:T(4,128)}, s32[1024]{0:T(1024)}, bf16[8,128,2048]{2,1,0:T(8,128)(2,1)}, f32[4,2048]{1,0:T(4,128)}, f32[4,2048]{1,0:T(4,128)}) %tuple.41, (f32[8,128,4,128]{3,2,1,0:T(4,128)}, f32[4,2048]{1,0:T(4,128)}, f32[4,2048]{1,0:T(4,128)}, ...), branch_computations={%region_0.17_spmd, %region_17.18_spmd} | conditional | flops 3166949632 | bytes 115961680 | solution.py:570
  3.1 1.4 %reshape.62.values = f32[64,128]{1,0:T(8,128)} reshape(f32[4,2048]{1,0:T(4,128)} %get-tuple-element.256) | data formatting | bytes 65536 | tf_op jit(solution)/shard_map/cond/branch_1_fun/reshape | solution.py:566
  4.5 1.4 %reshape.63.weights = f32[64,128]{1,0:T(8,128)} reshape(f32[4,2048]{1,0:T(4,128)} %get-tuple-element.257) | data formatting | bytes 65536 | tf_op jit(solution)/shard_map/cond/branch_1_fun/reshape | solution.py:566
  5.8 0.0 copy-start.1
  5.9 0.0 copy-start.6
  5.9 55.4 %analyse.1.recv = bf16[3,32,32,128]{3,2,1,0:T(8,128)(2,1)} custom-call(s32[32,128]{1,0:T(8,128)} %get-tuple-element.253.table, bf16[8,128,2048]{2,1,0:T(8,128)(2,1)} %get-tuple-element.255.obs_hbm, f32[4096,128]{1,0:T(8,128)} %bitcast.135, f32[64,128]{1,0:T(8,128)} %reshape.62.values, f32[64,128]{1,0:T(8,128)} %reshape.63.weights), custom_call_target="tpu_custom_call" | custom-call | tf_op jit(solution)/shard_map/cond/branch_1_fun/analyse/pallas_call | solution.py:492
  61.3 0.0 copy-done.1
  61.3 0.0 copy-done.6
  61.3 0.0 copy-start
  61.3 1.1 %copy-done = bf16[3,32,32,128]{3,2,1,0:T(8,128)(2,1)S(1)} copy-done((bf16[3,32,32,128]{3,2,1,0:T(8,128)(2,1)S(1)}, bf16[3,32,32,128]{3,2,1,0:T(8,128)(2,1)}, u32[]{:S(2)}) %copy-start) | copy-done | bytes 786456 | tf_op jit(solution)/shard_map/cond
  62.4 2.5 %scatter.1 = f32[4096,128]{1,0:T(8,128)S(1)} custom-call(s32[32,128]{1,0:T(8,128)S(1)} %copy-done.6, f32[4096,128]{1,0:T(8,128)S(1)} %bitcast.136, bf16[3,32,32,128]{3,2,1,0:T(8,128)(2,1)S(1)} %copy-done), custom_call_target="tpu_custom_call" | custom-call | tf_op jit(solution)/shard_map/cond/branch_1_fun/scatter/pallas_call | solution.py:550
  65.2 0.0 copy-start.3
  65.3 1.3 %copy-done.3 = f32[8,128,4,128]{3,2,1,0:T(4,128)} copy-done((f32[8,128,4,128]{3,2,1,0:T(4,128)}, f32[8,128,4,128]{3,2,1,0:T(4,128)S(1)}, u32[]{:S(2)}) %copy-start.3) | copy-done | bytes 2097176
Async XLA Ops:
  5.8 55.4 %copy-start.1 = (f32[8,128,4,128]{3,2,1,0:T(4,128)S(1)}, f32[8,128,4,128]{3,2,1,0:T(4,128)}, u32[]{:S(2)}) copy-start(f32[8,128,4,128]{3,2,1,0:T(4,128)} %get-tuple-element.254) | copy-start | bytes 6291460 | tf_op jit(solution)/shard_map/cond
  5.9 55.4 %copy-start.6 = (s32[32,128]{1,0:T(8,128)S(1)}, s32[32,128]{1,0:T(8,128)}, u32[]{:S(2)}) copy-start(s32[32,128]{1,0:T(8,128)} %get-tuple-element.253.table) | copy-start | bytes 49156 | tf_op jit(solution)/shard_map/cond
  61.3 1.1 %copy-start = (bf16[3,32,32,128]{3,2,1,0:T(8,128)(2,1)S(1)}, bf16[3,32,32,128]{3,2,1,0:T(8,128)(2,1)}, u32[]{:S(2)}) copy-start(bf16[3,32,32,128]{3,2,1,0:T(8,128)(2,1)} %analyse.1.recv) | copy-start | bytes 2359300 | tf_op jit(solution)/shard_map/cond
  65.2 1.3 %copy-start.3 = (f32[8,128,4,128]{3,2,1,0:T(4,128)}, f32[8,128,4,128]{3,2,1,0:T(4,128)S(1)}, u32[]{:S(2)}) copy-start(f32[8,128,4,128]{3,2,1,0:T(4,128)S(1)} %get-tuple-element.771) | copy-start | bytes 6291460

commit v3 on v2

--- a/solution.py
+++ b/solution.py
@@ -15,12 +15,12 @@
 SLOT_BLOCKS = 16
 HELD = 3
 CAPACITY = 24
-THIRD = 4
+THIRD = 6
 ROWS = 8
 ENS = 256
 CODE = 32767.0 / 6.0
 ROOT_CODE = 32767.0 / 0.708
-TILE_ROWS = 4 * SLOT_BLOCKS
+SIDE_ROWS = 8 * SLOT_BLOCKS
 AT_TILE, AT_BLOCKS, AT_COUNT = 32, 36, 64
 
 
@@ -118,7 +118,7 @@
     return lax.all_to_all(result, "ens", split_axis=0, concat_axis=1, tiled=True)
 
 
-def plan_kernel(counts, table, fits):
+def write_plan(counts, table, fits):
     lane = lax.broadcasted_iota(jnp.int32, (8, LANES), 1)
     device = lane % WAYS
     tiles = counts[...]
@@ -184,22 +184,6 @@
     table[...] = out
 
 
-def make_plan(obs_count):
-    return pl.pallas_call(
-        plan_kernel,
-        out_shape=(
-            jax.ShapeDtypeStruct((WAYS, LANES), jnp.int32),
-            jax.ShapeDtypeStruct((1, 1), jnp.int32),
-        ),
-        in_specs=[pl.BlockSpec(memory_space=pltpu.VMEM)],
-        out_specs=(
-            pl.BlockSpec(memory_space=pltpu.VMEM),
-            pl.BlockSpec(memory_space=pltpu.SMEM),
-        ),
-        name="plan",
-    )(obs_count.reshape(8, GROUP))
-
-
 def displacements():
     every = [(dx, dy, dc) for dx in range(4) for dy in range(4) for dc in range(2)][1:]
     return sorted(every, key=lambda d: -(min(d[0], 4 - d[0]) + min(d[1], 4 - d[1])))
@@ -250,23 +234,28 @@
 
 
 def analyse_kernel(
-    table, obs_hbm, mem_hbm, values, weights,
-    out_recv,
-    obs_in, wide, mem_in, obs_send, mem_send, side_send, obs_recv, mem_recv, side_recv, side,
+    counts, obs_hbm, mem_hbm, values, weights,
+    out_recv, plan, fits,
+    table, obs_in, wide, mem_in, obs_send, mem_send, side_send, obs_recv, mem_recv, side_recv, side,
     out_send, root, root_t,
-    in_sem, obs_ssem, obs_rsem, mem_ssem, mem_rsem, side_ssem, side_rsem, out_ssem, out_rsem, own_sem,
+    in_sem, side_ssem, side_rsem, phase_sem,
 ):
     me = lax.axis_index("ens")
     core = me % 2
     steps = displacements()
     targets = [shifted(me, step) for step in steps]
-    sources = [shifted(me, step, -1) for step in steps]
 
     def remote(src, dst, ssem, rsem, target):
         return pltpu.make_async_remote_copy(
             src_ref=src, dst_ref=dst, send_sem=ssem, recv_sem=rsem,
             device_id={"ens": target}, device_id_type=MESH,
         )
+
+    barrier = pltpu.get_barrier_semaphore()
+    for target in targets:
+        pl.semaphore_signal(barrier, inc=1, device_id={"ens": target}, device_id_type=MESH)
+    def drain(ref, sem):
+        pltpu.make_async_copy(ref, ref, sem).wait()
 
     mem_load = pltpu.make_async_copy(mem_hbm, mem_in, in_sem.at[ROWS])
     obs_loads = [
@@ -276,23 +265,29 @@
         copy.start()
     mem_load.start()
 
-    barrier = pltpu.get_barrier_semaphore()
-    for target in targets:
-        pl.semaphore_signal(barrier, inc=1, device_id={"ens": target}, device_id_type=MESH)
-    side_send[0:TILE_ROWS] = coded(values[...], CODE)
-    side_send[TILE_ROWS : 2 * TILE_ROWS] = coded(jnp.sqrt(weights[...]), ROOT_CODE)
+    parts = []
+    for part in range(SLOT_BLOCKS):
+        lanes = slice(part * LANES, (part + 1) * LANES)
+        parts += [values[:, lanes] * CODE, jnp.sqrt(weights[:, lanes]) * ROOT_CODE]
+    side_send[...] = coded(jnp.concatenate(parts, axis=0), 1.0)
+    write_plan(counts, plan, fits)
+    table_copy = pltpu.make_async_copy(plan, table, in_sem.at[ROWS + 1])
+    table_copy.start()
     pl.semaphore_wait(barrier, WAYS - 1)
 
+    x, y = me // 8, (me // 2) % 4
+    outer, inner = y + core * (x - y), x + core * (y - x)
     side_copies = []
-    for i, (step, target) in enumerate(zip(steps, targets)):
-        if step[2] == 0:
-            copy = remote(
-                side_send, side_recv.at[core, me // 2], side_ssem.at[i], side_rsem.at[i], target
-            )
-            copy.start()
-            side_copies.append(copy)
-    own_side = pltpu.make_async_copy(side_send, side_recv.at[core, me // 2], own_sem.at[0])
-    own_side.start()
+    for step in range(1, 4):
+        target = ((x + step * (1 - core)) % 4) * 8 + ((y + step * core) % 4) * 2 + core
+        copy = remote(
+            side_send, side_recv.at[core, outer, inner], side_ssem.at[step], side_rsem.at[step], target
+        )
+        copy.start()
+        side_copies.append(copy)
+    copy = pltpu.make_async_copy(side_send, side_recv.at[core, outer, inner], side_rsem.at[0])
+    copy.start()
+    side_copies.append(copy)
 
     for m in range(ROWS):
         obs_loads[m].wait()
@@ -304,6 +299,19 @@
             return carry
 
         lax.fori_loop(0, SLOT_BLOCKS, widen, 0)
+
+    for copy in side_copies:
+        copy.wait()
+    side_copies = []
+    for step in range(1, 4):
+        target = ((x + step * core) % 4) * 8 + ((y + step * (1 - core)) % 4) * 2 + core
+        copy = remote(
+            side_recv.at[core, outer], side_recv.at[core, outer],
+            side_ssem.at[3 + step], side_rsem.at[3 + step], target,
+        )
+        copy.start()
+        side_copies.append(copy)
+    table_copy.wait()
 
     def pack_obs(dest):
         for pair in range(CAPACITY // 2):
@@ -318,58 +326,57 @@
         parts = [mem_in[pl.ds(row + f, ROWS, stride=4 * GROUP), :] for f in range(4)]
         mem_send[slot, dest] = coded(jnp.concatenate(parts, axis=0), CODE)
 
-    obs_copies = []
-    for i, target in enumerate(targets):
+    for target in targets:
         pack_obs(target)
-        copy = remote(
-            obs_send.at[target], obs_recv.at[me], obs_ssem.at[i], obs_rsem.at[i], target
-        )
-        copy.start()
-        obs_copies.append(copy)
+        remote(
+            obs_send.at[target], obs_recv.at[me], phase_sem.at[0], phase_sem.at[1], target
+        ).start()
     pack_obs(me)
-    copy = pltpu.make_async_copy(obs_send.at[me], obs_recv.at[me], own_sem.at[1])
-    copy.start()
-    obs_copies.append(copy)
+    pltpu.make_async_copy(obs_send.at[me], obs_recv.at[me], phase_sem.at[1]).start()
 
     mem_load.wait()
-    mem_copies = []
     for slot in range(HELD):
-        for i, target in enumerate(targets):
+
+        def send_members(target, slot=slot):
+            remote(
+                mem_send.at[slot, target], mem_recv.at[slot, me],
+                phase_sem.at[2 + slot], phase_sem.at[5 + slot], target,
+            ).start()
+
+        def keep_members(slot=slot):
+            pltpu.make_async_copy(
+                mem_send.at[slot, me], mem_recv.at[slot, me], phase_sem.at[5 + slot]
+            ).start()
+
+        for target in targets:
             pack_members(target, slot)
-            copy = remote(
-                mem_send.at[slot, target], mem_recv.at[slot, me],
-                mem_ssem.at[slot, i], mem_rsem.at[slot, i], target,
-            )
-            mem_copies.append(copy)
             if slot < 2:
-                copy.start()
+                send_members(target)
             else:
-                pl.when(target % 2 == 0)(copy.start)
+                pl.when(target % 2 == 0)(functools.partial(send_members, target))
         pack_members(me, slot)
-        copy = pltpu.make_async_copy(
-            mem_send.at[slot, me], mem_recv.at[slot, me], own_sem.at[2 + slot]
-        )
-        copy.start()
-        mem_copies.append(copy)
+        if slot < 2:
+            keep_members()
+        else:
+            pl.when(core == 0)(keep_members)
 
     for copy in side_copies:
         copy.wait()
-    own_side.wait()
-    partner = me + 1 - 2 * core
     copy = remote(
-        side_recv.at[core], side_recv.at[core], side_ssem.at[WAYS - 1], side_rsem.at[WAYS - 1], partner
+        side_recv.at[core], side_recv.at[core], side_ssem.at[7], side_rsem.at[7], me + 1 - 2 * core
     )
     copy.start()
     copy.wait()
     for c in range(2):
-        for chip in range(WAYS // 2):
-            first = (chip * 2 + c) * 2 * TILE_ROWS
-            side[first : first + 2 * TILE_ROWS, :] = (
-                side_recv[c, chip].astype(jnp.int32).astype(jnp.float32)
-            )
-
-    for copy in obs_copies:
-        copy.wait()
+        for far in range(4):
+            for near in range(4):
+                chip = near * 4 + far if c == 0 else far * 4 + near
+                first = (chip * 2 + c) * SIDE_ROWS
+                side[first : first + SIDE_ROWS, :] = (
+                    side_recv[c, far, near].astype(jnp.int32).astype(jnp.float32)
+                )
+
+    drain(obs_recv, phase_sem.at[1])
     lane = lax.broadcasted_iota(jnp.int32, (1, LANES), 1)
     for block in range(CAPACITY):
         half = (block % 2) * ROWS
@@ -379,9 +386,9 @@
         mean = jnp.sum(seen, axis=0, keepdims=True) * (1.0 / ENS)
         source = table[me, block]
         tile, part = source % GROUP, source // GROUP
-        side_row = (tile // 4) * 2 * TILE_ROWS + (tile % 4) * SLOT_BLOCKS + part
+        side_row = (tile // 4) * SIDE_ROWS + part * 8 + tile % 4
         live = lane < table[me, AT_COUNT + block]
-        scale = side[pl.ds(side_row + TILE_ROWS, 1), :] * (1.0 / ROOT_CODE)
+        scale = side[pl.ds(side_row + 4, 1), :] * (1.0 / ROOT_CODE)
         scale = jnp.where(live, scale, 0.0)
         innov = scale * (side[pl.ds(side_row, 1), :] * (1.0 / CODE) - mean)
         rows = scale * (seen - mean)
@@ -435,17 +442,12 @@
         lower = jnp.concatenate([full[half:, :half], full[half:, half:] + diagonal], axis=1)
         weight_t.append(jnp.concatenate([upper, lower], axis=0).astype(jnp.bfloat16))
 
-    others = WAYS - 1
-    out_copies = []
+    half_ways = WAYS // 2
     for slot in range(HELD):
-        for i in range(others):
-            copy = mem_copies[slot * WAYS + i]
-            if slot < 2:
-                copy.wait()
-            else:
-                pl.when(targets[i] % 2 == 0)(copy.wait_send)
-                pl.when(core == 0)(copy.wait_recv)
-        mem_copies[slot * WAYS + others].wait()
+        if slot < 2:
+            drain(mem_recv.at[slot], phase_sem.at[5 + slot])
+        else:
+            pl.when(core == 0)(lambda: drain(mem_recv.at[2], phase_sem.at[7]))
         raw = decoded(mem_recv[slot], CODE)
         fields = [raw[:, f * ROWS : (f + 1) * ROWS, :].reshape(ENS, LANES) for f in range(4)]
         state = jnp.concatenate(fields, axis=1)
@@ -456,78 +458,85 @@
             result[:, f * LANES : (f + 1) * LANES].reshape(WAYS, ROWS, LANES) for f in range(4)
         ]
         out_send[slot] = jnp.concatenate(parts, axis=1).astype(jnp.bfloat16)
-        for i, target in enumerate(targets):
-            copy = remote(
-                out_send.at[slot, target], out_recv.at[slot, me],
-                out_ssem.at[slot, i], out_rsem.at[slot, i], target,
-            )
-            out_copies.append(copy)
-            if slot < 2:
-                copy.start()
-            else:
-                pl.when(core == 0)(copy.start)
-        copy = pltpu.make_async_copy(
-            out_send.at[slot, me], out_recv.at[slot, me], own_sem.at[2 + HELD + slot]
-        )
-        copy.start()
-        out_copies.append(copy)
-    for slot in range(HELD):
-        for i in range(others):
-            copy = out_copies[slot * WAYS + i]
-            if slot < 2:
-                copy.wait()
-            else:
-                pl.when(core == 0)(copy.wait_send)
-                pl.when(sources[i] % 2 == 0)(copy.wait_recv)
-        out_copies[slot * WAYS + others].wait()
-
-
-def exchange_and_analyse(table, obs_ens, members, values, weights):
+
+        def send_result(slot=slot):
+            for target in targets:
+                remote(
+                    out_send.at[slot, target], out_recv.at[slot, me],
+                    phase_sem.at[8 + slot], phase_sem.at[11 + slot], target,
+                ).start()
+            pltpu.make_async_copy(
+                out_send.at[slot, me], out_recv.at[slot, me], phase_sem.at[11 + slot]
+            ).start()
+
+        if slot < 2:
+            send_result()
+        else:
+            pl.when(core == 0)(send_result)
+
+    sent = pl.ds(0, WAYS - 1)
+    drain(obs_send.at[sent], phase_sem.at[0])
+    for slot in range(2):
+        drain(mem_send.at[slot, sent], phase_sem.at[2 + slot])
+        drain(out_send.at[slot, sent], phase_sem.at[8 + slot])
+        drain(out_recv.at[slot], phase_sem.at[11 + slot])
+    drain(mem_send.at[2, pl.ds(0, half_ways - 1)], phase_sem.at[4])
+    pl.when(core == 1)(lambda: drain(mem_send.at[2, 0], phase_sem.at[4]))
+    pl.when(core == 0)(lambda: drain(out_send.at[2, sent], phase_sem.at[10]))
+    drain(out_recv.at[2, pl.ds(0, half_ways)], phase_sem.at[13])
+
+
+def exchange_and_analyse(counts, obs_ens, members, values, weights):
     smem = pl.BlockSpec(memory_space=pltpu.SMEM)
     vmem = pl.BlockSpec(memory_space=pltpu.VMEM)
     anywhere = pl.BlockSpec(memory_space=pl.ANY)
-    others = WAYS - 1
     dma = pltpu.SemaphoreType.DMA
     pairs = CAPACITY // 2
     return pl.pallas_call(
         analyse_kernel,
-        out_shape=jax.ShapeDtypeStruct((HELD, WAYS, 32, LANES), jnp.bfloat16),
-        in_specs=[smem, anywhere, anywhere, vmem, vmem],
-        out_specs=anywhere,
+        out_shape=(
+            jax.ShapeDtypeStruct((HELD, WAYS, 32, LANES), jnp.bfloat16),
+            jax.ShapeDtypeStruct((WAYS, LANES), jnp.int32),
+            jax.ShapeDtypeStruct((1, 1), jnp.int32),
+        ),
+        in_specs=[vmem, anywhere, anywhere, vmem, vmem],
+        out_specs=(anywhere, vmem, smem),
         scratch_shapes=[
+            pltpu.SMEM((WAYS, LANES), jnp.int32),
             pltpu.VMEM((ROWS, GROUP, SLOT_BLOCKS * LANES), jnp.bfloat16),
             pltpu.VMEM((ROWS * SLOT_BLOCKS * GROUP, LANES), jnp.float32),
             pltpu.VMEM((ROWS * GROUP * 4, LANES), jnp.float32),
             pltpu.VMEM((WAYS, pairs, 16, LANES), jnp.bfloat16),
             pltpu.VMEM((HELD, WAYS, 32, LANES), jnp.int16),
-            pltpu.VMEM((2 * TILE_ROWS, LANES), jnp.int16),
+            pltpu.VMEM((SIDE_ROWS, LANES), jnp.int16),
             pltpu.VMEM((WAYS, pairs, 16, LANES), jnp.bfloat16),
             pltpu.VMEM((HELD, WAYS, 32, LANES), jnp.int16),
-            pltpu.VMEM((2, WAYS // 2, 2 * TILE_ROWS, LANES), jnp.int16),
-            pltpu.VMEM((WAYS * 2 * TILE_ROWS, LANES), jnp.float32),
+            pltpu.VMEM((2, 4, 4, SIDE_ROWS, LANES), jnp.int16),
+            pltpu.VMEM((WAYS * SIDE_ROWS, LANES), jnp.float32),
             pltpu.VMEM((HELD, WAYS, 32, LANES), jnp.bfloat16),
             pltpu.VMEM((ENS + 16, CAPACITY * LANES), jnp.bfloat16),
             pltpu.VMEM((CAPACITY * LANES, ENS), jnp.bfloat16),
-            dma((ROWS + 1,)),
-            dma((others,)),
-            dma((others,)),
-            dma((HELD, others)),
-            dma((HELD, others)),
-            dma((WAYS,)),
-            dma((WAYS,)),
-            dma((HELD, others)),
-            dma((HELD, others)),
-            dma((2 + 2 * HELD,)),
+            dma((ROWS + 2,)),
+            dma((8,)),
+            dma((8,)),
+            dma((14,)),
         ],
         compiler_params=pltpu.CompilerParams(
             collective_id=0, has_side_effects=True, vmem_limit_bytes=56 << 20
         ),
         name="analyse",
-    )(table, obs_ens, members, values, weights)
-
-
-def scatter_kernel(table, members, recv, out):
-    out[...] = members[...]
+    )(counts, obs_ens, members, values, weights)
+
+
+def scatter_kernel(table, members, recv_hbm, out_hbm, recv, out, sems):
+    loads = [
+        pltpu.make_async_copy(members, out, sems.at[0]),
+        pltpu.make_async_copy(recv_hbm, recv, sems.at[1]),
+    ]
+    for copy in loads:
+        copy.start()
+    for copy in loads:
+        copy.wait()
 
     def place(dest, carry):
         for slot in range(HELD):
@@ -542,33 +551,40 @@
         return carry
 
     lax.fori_loop(0, WAYS, place, 0)
+    store = pltpu.make_async_copy(out, out_hbm, sems.at[2])
+    store.start()
+    store.wait()
 
 
 def scatter(table, members, recv):
     smem = pl.BlockSpec(memory_space=pltpu.SMEM)
-    vmem = pl.BlockSpec(memory_space=pltpu.VMEM)
+    anywhere = pl.BlockSpec(memory_space=pl.ANY)
     return pl.pallas_call(
         scatter_kernel,
         out_shape=jax.ShapeDtypeStruct(members.shape, jnp.float32),
-        in_specs=[smem, vmem, vmem],
-        out_specs=vmem,
-        compiler_params=pltpu.CompilerParams(vmem_limit_bytes=40 << 20),
+        in_specs=[smem, anywhere, anywhere],
+        out_specs=anywhere,
+        scratch_shapes=[
+            pltpu.VMEM(recv.shape, recv.dtype),
+            pltpu.VMEM(members.shape, jnp.float32),
+            pltpu.SemaphoreType.DMA((3,)),
+        ],
+        compiler_params=pltpu.CompilerParams(vmem_limit_bytes=60 << 20),
         name="scatter",
     )(table, members, recv)
 
 
 def body(members, obs_ens, obs_count, obs_value, obs_weight):
-    table, fits = make_plan(obs_count)
-
-    def compact(members, obs_ens, obs_count, obs_value, obs_weight):
-        flat = members.reshape(-1, LANES)
-        recv = exchange_and_analyse(
-            table, obs_ens, flat, obs_value.reshape(-1, LANES), obs_weight.reshape(-1, LANES)
-        )
-        return scatter(table, flat, recv).reshape(members.shape)
-
+    flat = members.reshape(-1, LANES)
+    recv, table, fits = exchange_and_analyse(
+        obs_count.reshape(-1, GROUP), obs_ens, flat, obs_value, obs_weight
+    )
+    result = scatter(table, flat, recv).reshape(members.shape)
     return lax.cond(
-        fits[0, 0] > 0, compact, static_body, members, obs_ens, obs_count, obs_value, obs_weight
+        fits[0, 0] > 0,
+        lambda result, *_: result,
+        lambda _, *inputs: static_body(*inputs),
+        result, members, obs_ens, obs_count, obs_value, obs_weight,
     )
 
 

time: 66.9 us -> 61.5 us (0.919)
  local copies, waits for them, and re-layouts: 5.23 us -> 0.02 us
    reshape x2 -> x0, local copies, waits for them, and re-layouts: 2.78 us -> none  [the longest x1 1.39 us: compact(): obs_value.reshape(-1, LANES)]
    pallas_call x1, Pallas kernels: 2.52 us -> 5.22 us  [scatter(): pl.pallas_call(scatter_kernel, out_shape=jax.ShapeDtypeStruct(members.sha...]
    pallas_call x2 -> x1, Pallas kernels: 57.6 us -> 55.2 us  [exchange_and_analyse(): pl.pallas_call(analyse_kernel, out_shape=(jax.ShapeDtypeStruct((HELD, WAY...]
    unnamed x2 -> x6, local copies, waits for them, and re-layouts: 1.31 us -> 0.02 us
    cond x6 -> x0, local copies, waits for them, and re-layouts: 1.13 us -> none
where the time goes in v3:
time: 61.5 us; the launch traced here: 61.3 us
  Pallas kernels  60.4 us (98%)
  between operations  0.85 us (1%)
    pallas_call x1, Pallas kernels, exchange_and_analyse(): pl.pallas_call(analyse_kernel, out_shape=(jax.ShapeDtypeStruct((HELD, WAY...  55.2 us
    pallas_call x1, Pallas kernels, scatter(): pl.pallas_call(scatter_kernel, out_shape=jax.ShapeDtypeStruct(members.sha...  5.22 us

profile of v3, /device:TPU:1, one launch (start us, length us, event | category | flops | bytes accessed | tf_op | source)
XLA Modules:
  0.0 61.3 jit_solution(8867804447575821680)
XLA Ops:
  0.0 0.0 copy-start
  0.0 55.2 %analyse.1 = (bf16[3,32,32,128]{3,2,1,0:T(8,128)(2,1)}, s32[32,128]{1,0:T(8,128)}, s32[1,1]{1,0:T(1,128)}) custom-call(s32[8,128]{1,0:T(8,128)} %bitcast.164, bf16[8,128,2048]{2,1,0:T(8,128)(2,1)} %obs_hbm.1, f32[4096,128]{1,0:T(8,128)} %bitcast.136, f32[4,2048]{1,0:T(4,128)} %values.1, f32[4,2048]{1,0:T(4,128)} %weights.1), custom_call_target="tpu_custom_call" | custom-call | tf_op jit(solution)/shard_map/analyse/pallas_call | solution.py:495
  55.2 0.0 copy-done
  55.2 0.0 copy-start.2
  55.2 0.0 copy-start.3
  55.2 5.2 %scatter.1 = f32[4096,128]{1,0:T(8,128)} custom-call(s32[32,128]{1,0:T(8,128)} %get-tuple-element.250.table, f32[4096,128]{1,0:T(8,128)S(1)} %bitcast.137, bf16[3,32,32,128]{3,2,1,0:T(8,128)(2,1)} %get-tuple-element.251.recv_hbm), custom_call_target="tpu_custom_call" | custom-call | tf_op jit(solution)/shard_map/scatter/pallas_call | solution.py:562
  61.1 0.0 copy-done.2
  61.1 0.0 copy-done.3
  (1 shorter events, 0.0 us)
Async XLA Ops:
  0.0 55.2 %copy-start = (f32[8,128,4,128]{3,2,1,0:T(4,128)S(1)}, f32[8,128,4,128]{3,2,1,0:T(4,128)}, u32[]{:S(2)}) copy-start(f32[8,128,4,128]{3,2,1,0:T(4,128)} %param.19) | copy-start | bytes 6291460
  55.2 5.9 %copy-start.2 = (f32[4,2048]{1,0:T(4,128)S(1)}, f32[4,2048]{1,0:T(4,128)}, u32[]{:S(2)}) copy-start(f32[4,2048]{1,0:T(4,128)} %values.1) | copy-start | bytes 98308
  55.2 5.9 %copy-start.3 = (f32[4,2048]{1,0:T(4,128)S(1)}, f32[4,2048]{1,0:T(4,128)}, u32[]{:S(2)}) copy-start(f32[4,2048]{1,0:T(4,128)} %weights.1) | copy-start | bytes 98308

commit v4 on v3

--- a/solution.py
+++ b/solution.py
@@ -15,13 +15,14 @@
 SLOT_BLOCKS = 16
 HELD = 3
 CAPACITY = 24
+PART = 12
 THIRD = 6
 ROWS = 8
 ENS = 256
 CODE = 32767.0 / 6.0
 ROOT_CODE = 32767.0 / 0.708
 SIDE_ROWS = 8 * SLOT_BLOCKS
-AT_TILE, AT_BLOCKS, AT_COUNT = 32, 36, 64
+AT_TILE, AT_BLOCKS, AT_COUNT, AT_SIDE = 32, 36, 64, 96
 
 
 def solve_weights(gram_matrix, obs_vector):
@@ -136,7 +137,7 @@
         third = jnp.where(there == third_rank, value, third)
 
     def blocks_of(array):
-        return (array // GROUP + LANES - 1) // LANES
+        return ((array >> 7) + LANES - 1) >> 7
 
     pair = (blocks_of(first) + blocks_of(second)) * WAYS + device
     pair_rank = jnp.zeros_like(pair)
@@ -174,12 +175,17 @@
         return at_key, at_block
 
     at_key, at_block = table_of(wide_lane)
-    out = jnp.maximum(at_block, 0) * GROUP + at_key % GROUP
+    out = jnp.maximum(at_block, 0) * GROUP + (at_key & (GROUP - 1))
     at_key, at_block = table_of(wide_lane - AT_COUNT)
-    left = jnp.where(at_block >= 0, at_key // GROUP - at_block * LANES, 0)
+    left = jnp.where(at_block >= 0, (at_key >> 7) - at_block * LANES, 0)
     out = jnp.where(wide_lane >= AT_COUNT, left, out)
+    at_key, at_block = table_of(wide_lane - AT_SIDE)
+    tile = at_key & (GROUP - 1)
+    near = jnp.where(lax.axis_index("ens") % 2 == 0, tile >> 5, (tile >> 3) & 3)
+    side_row = near * SIDE_ROWS + jnp.maximum(at_block, 0) * 8 + (tile & 3)
+    out = jnp.where(wide_lane >= AT_SIDE, side_row, out)
     for slot in range(HELD):
-        out = jnp.where(wide_lane == AT_TILE + slot, keys[slot] % GROUP, out)
+        out = jnp.where(wide_lane == AT_TILE + slot, keys[slot] & (GROUP - 1), out)
         out = jnp.where(wide_lane == AT_BLOCKS + slot, size[slot], out)
     table[...] = out
 
@@ -236,9 +242,9 @@
 def analyse_kernel(
     counts, obs_hbm, mem_hbm, values, weights,
     out_recv, plan, fits,
-    table, obs_in, wide, mem_in, obs_send, mem_send, side_send, obs_recv, mem_recv, side_recv, side,
-    out_send, root, root_t,
-    in_sem, side_ssem, side_rsem, phase_sem,
+    table, obs_in, wide, mem_in, obs_send, mem_send, side_send, row_send, obs_recv, mem_recv,
+    side_recv, row_recv, side, rows, out_send, root, root_t, pert,
+    in_sem, phase_sem,
 ):
     me = lax.axis_index("ens")
     core = me % 2
@@ -276,18 +282,13 @@
     pl.semaphore_wait(barrier, WAYS - 1)
 
     x, y = me // 8, (me // 2) % 4
-    outer, inner = y + core * (x - y), x + core * (y - x)
-    side_copies = []
+    near = x + core * (y - x)
     for step in range(1, 4):
         target = ((x + step * (1 - core)) % 4) * 8 + ((y + step * core) % 4) * 2 + core
-        copy = remote(
-            side_send, side_recv.at[core, outer, inner], side_ssem.at[step], side_rsem.at[step], target
-        )
-        copy.start()
-        side_copies.append(copy)
-    copy = pltpu.make_async_copy(side_send, side_recv.at[core, outer, inner], side_rsem.at[0])
-    copy.start()
-    side_copies.append(copy)
+        remote(
+            side_send, side_recv.at[near], phase_sem.at[14], phase_sem.at[15], target
+        ).start()
+    pltpu.make_async_copy(side_send, side_recv.at[near], phase_sem.at[15]).start()
 
     for m in range(ROWS):
         obs_loads[m].wait()
@@ -300,39 +301,58 @@
 
         lax.fori_loop(0, SLOT_BLOCKS, widen, 0)
 
-    for copy in side_copies:
-        copy.wait()
-    side_copies = []
-    for step in range(1, 4):
-        target = ((x + step * core) % 4) * 8 + ((y + step * (1 - core)) % 4) * 2 + core
-        copy = remote(
-            side_recv.at[core, outer], side_recv.at[core, outer],
-            side_ssem.at[3 + step], side_rsem.at[3 + step], target,
-        )
-        copy.start()
-        side_copies.append(copy)
     table_copy.wait()
 
-    def pack_obs(dest):
-        for pair in range(CAPACITY // 2):
+    def pack_obs(dest, part):
+        for pair in range(PART // 2):
+            at = part * PART + 2 * pair
             rows = [
-                wide[pl.ds(table[dest, 2 * pair + j], ROWS, stride=SLOT_BLOCKS * GROUP), :]
+                wide[pl.ds(table[dest, at + j], ROWS, stride=SLOT_BLOCKS * GROUP), :]
                 for j in range(2)
             ]
-            obs_send[dest, pair] = jnp.concatenate(rows, axis=0).astype(jnp.bfloat16)
+            obs_send[part, dest, pair] = jnp.concatenate(rows, axis=0).astype(jnp.bfloat16)
+
+    def send_obs(part):
+        for target in targets:
+            pack_obs(target, part)
+            remote(
+                obs_send.at[part, target], obs_recv.at[part, me],
+                phase_sem.at[part], phase_sem.at[16 + part], target,
+            ).start()
+        pack_obs(me, part)
+        pltpu.make_async_copy(
+            obs_send.at[part, me], obs_recv.at[part, me], phase_sem.at[16 + part]
+        ).start()
 
     def pack_members(dest, slot):
         row = table[dest, AT_TILE + slot] * 4
         parts = [mem_in[pl.ds(row + f, ROWS, stride=4 * GROUP), :] for f in range(4)]
         mem_send[slot, dest] = coded(jnp.concatenate(parts, axis=0), CODE)
 
-    for target in targets:
-        pack_obs(target)
-        remote(
-            obs_send.at[target], obs_recv.at[me], phase_sem.at[0], phase_sem.at[1], target
-        ).start()
-    pack_obs(me)
-    pltpu.make_async_copy(obs_send.at[me], obs_recv.at[me], phase_sem.at[1]).start()
+    send_obs(0)
+
+    drain(side_recv, phase_sem.at[15])
+    side[...] = side_recv[...].reshape(4 * SIDE_ROWS, LANES).astype(jnp.int32).astype(jnp.float32)
+    own_slot = y + core * (4 + x - y)
+    for step in range(4):
+        for other in range(2):
+            dest = ((x + step * core) % 4) * 8 + ((y + step * (1 - core)) % 4) * 2
+            dest = dest + (core + other) % 2
+            picked = [
+                side[pl.ds(table[dest, AT_SIDE + block], 2, stride=4), :] for block in range(CAPACITY)
+            ]
+            at = step * 2 + other
+            row_send[at] = coded(jnp.concatenate(picked, axis=0), 1.0)
+            if at:
+                remote(
+                    row_send.at[at], row_recv.at[own_slot], phase_sem.at[18], phase_sem.at[19], dest
+                ).start()
+            else:
+                pltpu.make_async_copy(
+                    row_send.at[at], row_recv.at[own_slot], phase_sem.at[19]
+                ).start()
+
+    send_obs(1)
 
     mem_load.wait()
     for slot in range(HELD):
@@ -360,41 +380,29 @@
         else:
             pl.when(core == 0)(keep_members)
 
-    for copy in side_copies:
-        copy.wait()
-    copy = remote(
-        side_recv.at[core], side_recv.at[core], side_ssem.at[7], side_rsem.at[7], me + 1 - 2 * core
-    )
-    copy.start()
-    copy.wait()
-    for c in range(2):
-        for far in range(4):
-            for near in range(4):
-                chip = near * 4 + far if c == 0 else far * 4 + near
-                first = (chip * 2 + c) * SIDE_ROWS
-                side[first : first + SIDE_ROWS, :] = (
-                    side_recv[c, far, near].astype(jnp.int32).astype(jnp.float32)
-                )
-
-    drain(obs_recv, phase_sem.at[1])
+    drain(row_recv, phase_sem.at[19])
+    rows[...] = row_recv[...].reshape(8 * 2 * CAPACITY, LANES).astype(jnp.int32).astype(jnp.float32)
+
     lane = lax.broadcasted_iota(jnp.int32, (1, LANES), 1)
-    for block in range(CAPACITY):
-        half = (block % 2) * ROWS
+
+    def form_roots(block):
+        part, place = block // PART, block % PART
+        half = (place % 2) * ROWS
         columns = pl.ds(block * LANES, LANES)
-        seen = obs_recv[:, block // 2].astype(jnp.float32)[:, half : half + ROWS, :]
+        seen = obs_recv[part, :, place // 2].astype(jnp.float32)[:, half : half + ROWS, :]
         seen = seen.reshape(ENS, LANES)
         mean = jnp.sum(seen, axis=0, keepdims=True) * (1.0 / ENS)
-        source = table[me, block]
-        tile, part = source % GROUP, source // GROUP
-        side_row = (tile // 4) * SIDE_ROWS + part * 8 + tile % 4
+        owner = (table[me, block] & (GROUP - 1)) >> 2
+        owner_core = owner & 1
+        slot = (1 - owner_core) * ((owner >> 1) & 3) + owner_core * (4 + (owner >> 3))
+        pair = rows[pl.ds(slot * 2 * CAPACITY + 2 * block, 2), :]
         live = lane < table[me, AT_COUNT + block]
-        scale = side[pl.ds(side_row + 4, 1), :] * (1.0 / ROOT_CODE)
-        scale = jnp.where(live, scale, 0.0)
-        innov = scale * (side[pl.ds(side_row, 1), :] * (1.0 / CODE) - mean)
-        rows = scale * (seen - mean)
-        root[0:ENS, columns] = rows.astype(jnp.bfloat16)
+        scale = jnp.where(live, pair[1:2] * (1.0 / ROOT_CODE), 0.0)
+        innov = scale * (pair[0:1] * (1.0 / CODE) - mean)
+        scaled = scale * (seen - mean)
+        root[0:ENS, columns] = scaled.astype(jnp.bfloat16)
         root[ENS : ENS + 16, columns] = jnp.broadcast_to(innov, (16, LANES)).astype(jnp.bfloat16)
-        root_t[block * LANES : (block + 1) * LANES, :] = rows.T.astype(jnp.bfloat16)
+        root_t[block * LANES : (block + 1) * LANES, :] = scaled.T.astype(jnp.bfloat16)
 
     reach = [
         (0, SLOT_BLOCKS),
@@ -410,14 +418,29 @@
     ).astype(jnp.float32)
     held = range(HELD)
     vecs, bounds, ys = [], [], []
-    for slot in held:
-        low, high = reach[slot]
+
+    def sums_of(slot, part):
+        low, high = max(reach[slot][0], part * PART), min(reach[slot][1], (part + 1) * PART)
+        if low >= high:
+            return None
         place = low + lax.broadcasted_iota(jnp.int32, (1, (high - low) * LANES), 1) // LANES
         mine = (place >= start[slot]) & (place < start[slot] + size[slot])
-        part = root[:, low * LANES : high * LANES] * mine.astype(jnp.float32).astype(jnp.bfloat16)
-        sums = jnp.dot(
-            part, root_t[low * LANES : high * LANES, :], preferred_element_type=jnp.float32
+        masked = root[:, low * LANES : high * LANES] * mine.astype(jnp.float32).astype(jnp.bfloat16)
+        return jnp.dot(
+            masked, root_t[low * LANES : high * LANES, :], preferred_element_type=jnp.float32
         )
+
+    drain(obs_recv.at[0], phase_sem.at[16])
+    for block in range(PART):
+        form_roots(block)
+    early = [sums_of(slot, 0) for slot in held]
+    drain(obs_recv.at[1], phase_sem.at[17])
+    for block in range(PART, CAPACITY):
+        form_roots(block)
+    for slot in held:
+        sums = sums_of(slot, 1)
+        if early[slot] is not None:
+            sums = sums + early[slot]
         gram = sums[0:ENS]
         vecs.append(sums[ENS : ENS + 8])
         trace = jnp.sum((gram[:half, :half] + gram[half:, half:]) * eye)
@@ -426,7 +449,23 @@
         ys.append(centred((ENS - 1.0) / bound, gram * (1.0 / bound), eye))
     zs = middles = [middle_of(y) for y in ys]
     ys = [times(ys[slot], middles[slot], eye) for slot in held]
+
+    def centre_members(slot):
+        if slot < 2:
+            drain(mem_recv.at[slot], phase_sem.at[5 + slot])
+        else:
+            pl.when(core == 0)(lambda: drain(mem_recv.at[2], phase_sem.at[7]))
+        raw = decoded(mem_recv[slot], CODE)
+        fields = [raw[:, f * ROWS : (f + 1) * ROWS, :].reshape(ENS, LANES) for f in range(4)]
+        state = jnp.concatenate(fields, axis=1)
+        mean = jnp.sum(state, axis=0, keepdims=True) * (1.0 / ENS)
+        pert[slot] = (state - mean).astype(jnp.bfloat16)
+        return mean
+
+    means = []
     for iteration in range(1, NEWTON):
+        if iteration >= 3:
+            means.append(centre_members(iteration - 3))
         middles = [middle_of(times(zs[slot], ys[slot], eye)) for slot in held]
         if iteration < NEWTON - 1:
             ys = [times(ys[slot], middles[slot], eye) for slot in held]
@@ -444,16 +483,10 @@
 
     half_ways = WAYS // 2
     for slot in range(HELD):
-        if slot < 2:
-            drain(mem_recv.at[slot], phase_sem.at[5 + slot])
-        else:
-            pl.when(core == 0)(lambda: drain(mem_recv.at[2], phase_sem.at[7]))
-        raw = decoded(mem_recv[slot], CODE)
-        fields = [raw[:, f * ROWS : (f + 1) * ROWS, :].reshape(ENS, LANES) for f in range(4)]
-        state = jnp.concatenate(fields, axis=1)
-        mean = jnp.sum(state, axis=0, keepdims=True) * (1.0 / ENS)
-        pert = (state - mean).astype(jnp.bfloat16)
-        result = mean + jnp.dot(weight_t[slot], pert, preferred_element_type=jnp.float32)
+        if slot == 2:
+            means.append(centre_members(2))
+        result = jnp.dot(weight_t[slot], pert[slot], preferred_element_type=jnp.float32)
+        result = means[slot] + result
         parts = [
             result[:, f * LANES : (f + 1) * LANES].reshape(WAYS, ROWS, LANES) for f in range(4)
         ]
@@ -475,7 +508,10 @@
             pl.when(core == 0)(send_result)
 
     sent = pl.ds(0, WAYS - 1)
-    drain(obs_send.at[sent], phase_sem.at[0])
+    for part in range(2):
+        drain(obs_send.at[part, sent], phase_sem.at[part])
+    drain(side_recv.at[pl.ds(0, 3)], phase_sem.at[14])
+    drain(row_send.at[pl.ds(0, 7)], phase_sem.at[18])
     for slot in range(2):
         drain(mem_send.at[slot, sent], phase_sem.at[2 + slot])
         drain(out_send.at[slot, sent], phase_sem.at[8 + slot])
@@ -491,7 +527,6 @@
     vmem = pl.BlockSpec(memory_space=pltpu.VMEM)
     anywhere = pl.BlockSpec(memory_space=pl.ANY)
     dma = pltpu.SemaphoreType.DMA
-    pairs = CAPACITY // 2
     return pl.pallas_call(
         analyse_kernel,
         out_shape=(
@@ -506,20 +541,22 @@
             pltpu.VMEM((ROWS, GROUP, SLOT_BLOCKS * LANES), jnp.bfloat16),
             pltpu.VMEM((ROWS * SLOT_BLOCKS * GROUP, LANES), jnp.float32),
             pltpu.VMEM((ROWS * GROUP * 4, LANES), jnp.float32),
-            pltpu.VMEM((WAYS, pairs, 16, LANES), jnp.bfloat16),
+            pltpu.VMEM((2, WAYS, PART // 2, 16, LANES), jnp.bfloat16),
             pltpu.VMEM((HELD, WAYS, 32, LANES), jnp.int16),
             pltpu.VMEM((SIDE_ROWS, LANES), jnp.int16),
-            pltpu.VMEM((WAYS, pairs, 16, LANES), jnp.bfloat16),
+            pltpu.VMEM((8, 2 * CAPACITY, LANES), jnp.int16),
+            pltpu.VMEM((2, WAYS, PART // 2, 16, LANES), jnp.bfloat16),
             pltpu.VMEM((HELD, WAYS, 32, LANES), jnp.int16),
-            pltpu.VMEM((2, 4, 4, SIDE_ROWS, LANES), jnp.int16),
-            pltpu.VMEM((WAYS * SIDE_ROWS, LANES), jnp.float32),
+            pltpu.VMEM((4, SIDE_ROWS, LANES), jnp.int16),
+            pltpu.VMEM((8, 2 * CAPACITY, LANES), jnp.int16),
+            pltpu.VMEM((4 * SIDE_ROWS, LANES), jnp.float32),
+            pltpu.VMEM((16 * CAPACITY, LANES), jnp.float32),
             pltpu.VMEM((HELD, WAYS, 32, LANES), jnp.bfloat16),
             pltpu.VMEM((ENS + 16, CAPACITY * LANES), jnp.bfloat16),
             pltpu.VMEM((CAPACITY * LANES, ENS), jnp.bfloat16),
+            pltpu.VMEM((HELD, ENS, 4 * LANES), jnp.bfloat16),
             dma((ROWS + 2,)),
-            dma((8,)),
-            dma((8,)),
-            dma((14,)),
+            dma((20,)),
         ],
         compiler_params=pltpu.CompilerParams(
             collective_id=0, has_side_effects=True, vmem_limit_bytes=56 << 20

time: 61.5 us -> 55 us (0.89)
  Pallas kernels: 60.4 us -> 53.9 us
    pallas_call x1, Pallas kernels: 55.2 us -> 48.6 us  [exchange_and_analyse(): pl.pallas_call(analyse_kernel, out_shape=(jax.ShapeDtypeStruct((HELD, WAY...]
where the time goes in v4:
time: 55 us; the launch traced here: 54.8 us
  Pallas kernels  53.9 us (98%)
  between operations  0.85 us (2%)
    pallas_call x1, Pallas kernels, exchange_and_analyse(): pl.pallas_call(analyse_kernel, out_shape=(jax.ShapeDtypeStruct((HELD, WAY...  48.6 us
    pallas_call x1, Pallas kernels, scatter(): pl.pallas_call(scatter_kernel, out_shape=jax.ShapeDtypeStruct(members.sha...  5.28 us

profile of v4, /device:TPU:1, one launch (start us, length us, event | category | flops | bytes accessed | tf_op | source)
XLA Modules:
  0.0 54.8 jit_solution(13752520253219974576)
XLA Ops:
  0.0 0.0 copy-start
  0.0 48.6 %analyse.1 = (bf16[3,32,32,128]{3,2,1,0:T(8,128)(2,1)}, s32[32,128]{1,0:T(8,128)}, s32[1,1]{1,0:T(1,128)}) custom-call(s32[8,128]{1,0:T(8,128)} %bitcast.164, bf16[8,128,2048]{2,1,0:T(8,128)(2,1)} %obs_hbm.1, f32[4096,128]{1,0:T(8,128)} %bitcast.136, f32[4,2048]{1,0:T(4,128)} %values.1, f32[4,2048]{1,0:T(4,128)} %weights.1), custom_call_target="tpu_custom_call" | custom-call | tf_op jit(solution)/shard_map/analyse/pallas_call | solution.py:530
  48.6 0.0 copy-done
  48.7 0.0 copy-start.2
  48.7 0.0 copy-start.3
  48.7 5.3 %scatter.1 = f32[4096,128]{1,0:T(8,128)} custom-call(s32[32,128]{1,0:T(8,128)} %get-tuple-element.250.table, f32[4096,128]{1,0:T(8,128)S(1)} %bitcast.137, bf16[3,32,32,128]{3,2,1,0:T(8,128)(2,1)} %get-tuple-element.251.recv_hbm), custom_call_target="tpu_custom_call" | custom-call | tf_op jit(solution)/shard_map/scatter/pallas_call | solution.py:599
  54.6 0.0 copy-done.2
  54.6 0.0 copy-done.3
  (1 shorter events, 0.0 us)
Async XLA Ops:
  0.0 48.6 %copy-start = (f32[8,128,4,128]{3,2,1,0:T(4,128)S(1)}, f32[8,128,4,128]{3,2,1,0:T(4,128)}, u32[]{:S(2)}) copy-start(f32[8,128,4,128]{3,2,1,0:T(4,128)} %param.19) | copy-start | bytes 6291460
  48.7 5.9 %copy-start.2 = (f32[4,2048]{1,0:T(4,128)S(1)}, f32[4,2048]{1,0:T(4,128)}, u32[]{:S(2)}) copy-start(f32[4,2048]{1,0:T(4,128)} %values.1) | copy-start | bytes 98308
  48.7 5.9 %copy-start.3 = (f32[4,2048]{1,0:T(4,128)S(1)}, f32[4,2048]{1,0:T(4,128)}, u32[]{:S(2)}) copy-start(f32[4,2048]{1,0:T(4,128)} %weights.1) | copy-start | bytes 98308

commit v5 on v4

--- a/solution.py
+++ b/solution.py
@@ -17,6 +17,7 @@
 CAPACITY = 24
 PART = 12
 THIRD = 6
+CHUNKS = 4
 ROWS = 8
 ENS = 256
 CODE = 32767.0 / 6.0
@@ -187,7 +188,12 @@
     for slot in range(HELD):
         out = jnp.where(wide_lane == AT_TILE + slot, keys[slot] & (GROUP - 1), out)
         out = jnp.where(wide_lane == AT_BLOCKS + slot, size[slot], out)
-    table[...] = out
+    table[0:WAYS, :] = out
+    found = jnp.zeros_like(wide_lane)
+    for slot in range(HELD):
+        hit = (keys[slot] & (GROUP - 1) == wide_lane) & (size[slot] > 0)
+        found += jnp.where(hit, slot * WAYS + wide_row + 1, 0)
+    table[WAYS : WAYS + 8, :] = jnp.broadcast_to(jnp.sum(found, axis=0, keepdims=True), (8, LANES))
 
 
 def displacements():
@@ -279,6 +285,17 @@
     write_plan(counts, plan, fits)
     table_copy = pltpu.make_async_copy(plan, table, in_sem.at[ROWS + 1])
     table_copy.start()
+    for m in range(ROWS):
+        obs_loads[m].wait()
+
+        def widen(block, carry):
+            first = pl.multiple_of((m * SLOT_BLOCKS + block) * GROUP, GROUP)
+            lanes = pl.ds(pl.multiple_of(block * LANES, LANES), LANES)
+            wide[pl.ds(first, GROUP), :] = obs_in[m, :, lanes].astype(jnp.float32)
+            return carry
+
+        lax.fori_loop(0, SLOT_BLOCKS, widen, 0)
+
     pl.semaphore_wait(barrier, WAYS - 1)
 
     x, y = me // 8, (me // 2) % 4
@@ -289,17 +306,6 @@
             side_send, side_recv.at[near], phase_sem.at[14], phase_sem.at[15], target
         ).start()
     pltpu.make_async_copy(side_send, side_recv.at[near], phase_sem.at[15]).start()
-
-    for m in range(ROWS):
-        obs_loads[m].wait()
-
-        def widen(block, carry):
-            first = pl.multiple_of((m * SLOT_BLOCKS + block) * GROUP, GROUP)
-            lanes = pl.ds(pl.multiple_of(block * LANES, LANES), LANES)
-            wide[pl.ds(first, GROUP), :] = obs_in[m, :, lanes].astype(jnp.float32)
-            return carry
-
-        lax.fori_loop(0, SLOT_BLOCKS, widen, 0)
 
     table_copy.wait()
 
@@ -417,7 +423,6 @@
         == lax.broadcasted_iota(jnp.int32, (half, half), 1)
     ).astype(jnp.float32)
     held = range(HELD)
-    vecs, bounds, ys = [], [], []
 
     def sums_of(slot, part):
         low, high = max(reach[slot][0], part * PART), min(reach[slot][1], (part + 1) * PART)
@@ -437,18 +442,6 @@
     drain(obs_recv.at[1], phase_sem.at[17])
     for block in range(PART, CAPACITY):
         form_roots(block)
-    for slot in held:
-        sums = sums_of(slot, 1)
-        if early[slot] is not None:
-            sums = sums + early[slot]
-        gram = sums[0:ENS]
-        vecs.append(sums[ENS : ENS + 8])
-        trace = jnp.sum((gram[:half, :half] + gram[half:, half:]) * eye)
-        bound = (ENS - 1.0) + trace
-        bounds.append(bound)
-        ys.append(centred((ENS - 1.0) / bound, gram * (1.0 / bound), eye))
-    zs = middles = [middle_of(y) for y in ys]
-    ys = [times(ys[slot], middles[slot], eye) for slot in held]
 
     def centre_members(slot):
         if slot < 2:
@@ -462,50 +455,61 @@
         pert[slot] = (state - mean).astype(jnp.bfloat16)
         return mean
 
-    means = []
-    for iteration in range(1, NEWTON):
-        if iteration >= 3:
-            means.append(centre_members(iteration - 3))
-        middles = [middle_of(times(zs[slot], ys[slot], eye)) for slot in held]
-        if iteration < NEWTON - 1:
-            ys = [times(ys[slot], middles[slot], eye) for slot in held]
-        zs = [times(middles[slot], zs[slot], eye) for slot in held]
-    weight_t = []
-    for slot in held:
-        z, bound = zs[slot], bounds[slot]
-        shift = row_times(row_times(vecs[slot], z), z)[0:1] * (1.0 / bound)
-        factor = jnp.sqrt(jnp.float32(ENS - 1.0)) / jnp.sqrt(bound)
-        diagonal = (factor * z[0]) * eye
-        full = factor * z[1] + shift
-        upper = jnp.concatenate([full[:half, :half] + diagonal, full[:half, half:]], axis=1)
-        lower = jnp.concatenate([full[half:, :half], full[half:, half:] + diagonal], axis=1)
-        weight_t.append(jnp.concatenate([upper, lower], axis=0).astype(jnp.bfloat16))
+    def weights_of(slots):
+        vecs, bounds, ys, means = [], [], [], []
+        for slot in slots:
+            sums = sums_of(slot, 1)
+            if early[slot] is not None:
+                sums = sums + early[slot]
+            gram = sums[0:ENS]
+            vecs.append(sums[ENS : ENS + 8])
+            trace = jnp.sum((gram[:half, :half] + gram[half:, half:]) * eye)
+            bound = (ENS - 1.0) + trace
+            bounds.append(bound)
+            ys.append(centred((ENS - 1.0) / bound, gram * (1.0 / bound), eye))
+        zs = middles = [middle_of(y) for y in ys]
+        ys = [times(y, middle, eye) for y, middle in zip(ys, middles)]
+        for iteration in range(1, NEWTON):
+            if NEWTON - iteration <= len(slots):
+                means.append(centre_members(slots[len(means)]))
+            middles = [middle_of(times(z, y, eye)) for z, y in zip(zs, ys)]
+            if iteration < NEWTON - 1:
+                ys = [times(y, middle, eye) for y, middle in zip(ys, middles)]
+            zs = [times(middle, z, eye) for middle, z in zip(middles, zs)]
+        out = []
+        for z, bound, vec in zip(zs, bounds, vecs):
+            shift = row_times(row_times(vec, z), z)[0:1] * (1.0 / bound)
+            factor = jnp.sqrt(jnp.float32(ENS - 1.0)) / jnp.sqrt(bound)
+            diagonal = (factor * z[0]) * eye
+            full = factor * z[1] + shift
+            upper = jnp.concatenate([full[:half, :half] + diagonal, full[:half, half:]], axis=1)
+            lower = jnp.concatenate([full[half:, :half], full[half:, half:] + diagonal], axis=1)
+            out.append(jnp.concatenate([upper, lower], axis=0).astype(jnp.bfloat16))
+        return out, means
 
     half_ways = WAYS // 2
-    for slot in range(HELD):
-        if slot == 2:
-            means.append(centre_members(2))
-        result = jnp.dot(weight_t[slot], pert[slot], preferred_element_type=jnp.float32)
-        result = means[slot] + result
-        parts = [
-            result[:, f * LANES : (f + 1) * LANES].reshape(WAYS, ROWS, LANES) for f in range(4)
-        ]
-        out_send[slot] = jnp.concatenate(parts, axis=1).astype(jnp.bfloat16)
-
-        def send_result(slot=slot):
-            for target in targets:
-                remote(
-                    out_send.at[slot, target], out_recv.at[slot, me],
-                    phase_sem.at[8 + slot], phase_sem.at[11 + slot], target,
+    for slots in ((0, 1), (2,)):
+        for slot, weight_t, mean in zip(slots, *weights_of(slots)):
+            result = mean + jnp.dot(weight_t, pert[slot], preferred_element_type=jnp.float32)
+            parts = [
+                result[:, f * LANES : (f + 1) * LANES].reshape(WAYS, ROWS, LANES) for f in range(4)
+            ]
+            out_send[slot] = jnp.concatenate(parts, axis=1).astype(jnp.bfloat16)
+
+            def send_result(slot=slot):
+                for target in targets:
+                    remote(
+                        out_send.at[slot, target], out_recv.at[slot, me],
+                        phase_sem.at[8 + slot], phase_sem.at[11 + slot], target,
+                    ).start()
+                pltpu.make_async_copy(
+                    out_send.at[slot, me], out_recv.at[slot, me], phase_sem.at[11 + slot]
                 ).start()
-            pltpu.make_async_copy(
-                out_send.at[slot, me], out_recv.at[slot, me], phase_sem.at[11 + slot]
-            ).start()
-
-        if slot < 2:
-            send_result()
-        else:
-            pl.when(core == 0)(send_result)
+
+            if slot < 2:
+                send_result()
+            else:
+                pl.when(core == 0)(send_result)
 
     sent = pl.ds(0, WAYS - 1)
     for part in range(2):
@@ -531,13 +535,13 @@
         analyse_kernel,
         out_shape=(
             jax.ShapeDtypeStruct((HELD, WAYS, 32, LANES), jnp.bfloat16),
-            jax.ShapeDtypeStruct((WAYS, LANES), jnp.int32),
+            jax.ShapeDtypeStruct((WAYS + 8, LANES), jnp.int32),
             jax.ShapeDtypeStruct((1, 1), jnp.int32),
         ),
         in_specs=[vmem, anywhere, anywhere, vmem, vmem],
         out_specs=(anywhere, vmem, smem),
         scratch_shapes=[
-            pltpu.SMEM((WAYS, LANES), jnp.int32),
+            pltpu.SMEM((WAYS + 8, LANES), jnp.int32),
             pltpu.VMEM((ROWS, GROUP, SLOT_BLOCKS * LANES), jnp.bfloat16),
             pltpu.VMEM((ROWS * SLOT_BLOCKS * GROUP, LANES), jnp.float32),
             pltpu.VMEM((ROWS * GROUP * 4, LANES), jnp.float32),
@@ -566,31 +570,46 @@
 
 
 def scatter_kernel(table, members, recv_hbm, out_hbm, recv, out, sems):
+    width = 4 * GROUP // CHUNKS
+    recv_load = pltpu.make_async_copy(recv_hbm, recv, sems.at[0])
+    recv_load.start()
+
+    members = members.reshape(ROWS, 4 * GROUP, LANES)
+    out_hbm = out_hbm.reshape(ROWS, 4 * GROUP, LANES)
+
+    def rows(chunk):
+        return pl.ds(chunk * width, width)
+
     loads = [
-        pltpu.make_async_copy(members, out, sems.at[0]),
-        pltpu.make_async_copy(recv_hbm, recv, sems.at[1]),
+        pltpu.make_async_copy(members.at[:, rows(c)], out.at[c], sems.at[1 + c])
+        for c in range(CHUNKS)
+    ]
+    stores = [
+        pltpu.make_async_copy(out.at[c], out_hbm.at[:, rows(c)], sems.at[1 + CHUNKS + c])
+        for c in range(CHUNKS)
     ]
     for copy in loads:
         copy.start()
-    for copy in loads:
+    recv_load.wait()
+    for c in range(CHUNKS):
+        loads[c].wait()
+        flat = out.at[c].reshape(ROWS * width, LANES)
+
+        def place(index, carry):
+            at = table[WAYS, c * (GROUP // CHUNKS) + index]
+
+            @pl.when(at > 0)
+            def _():
+                tall = recv[at - 1].astype(jnp.float32)
+                for f in range(4):
+                    flat[pl.ds(index * 4 + f, ROWS, stride=width), :] = tall[f * ROWS : (f + 1) * ROWS]
+
+            return carry
+
+        lax.fori_loop(0, GROUP // CHUNKS, place, 0, unroll=4)
+        stores[c].start()
+    for copy in stores:
         copy.wait()
-
-    def place(dest, carry):
-        for slot in range(HELD):
-            row = table[dest, AT_TILE + slot] * 4
-
-            @pl.when(table[dest, AT_BLOCKS + slot] > 0)
-            def _():
-                tall = recv[slot, dest].astype(jnp.float32)
-                for f in range(4):
-                    out[pl.ds(row + f, ROWS, stride=4 * GROUP), :] = tall[f * ROWS : (f + 1) * ROWS]
-
-        return carry
-
-    lax.fori_loop(0, WAYS, place, 0)
-    store = pltpu.make_async_copy(out, out_hbm, sems.at[2])
-    store.start()
-    store.wait()
 
 
 def scatter(table, members, recv):
@@ -603,8 +622,8 @@
         out_specs=anywhere,
         scratch_shapes=[
             pltpu.VMEM(recv.shape, recv.dtype),
-            pltpu.VMEM(members.shape, jnp.float32),
-            pltpu.SemaphoreType.DMA((3,)),
+            pltpu.VMEM((CHUNKS, ROWS, 4 * GROUP // CHUNKS, LANES), jnp.float32),
+            pltpu.SemaphoreType.DMA((1 + 2 * CHUNKS,)),
         ],
         compiler_params=pltpu.CompilerParams(vmem_limit_bytes=60 << 20),
         name="scatter",
@@ -616,6 +635,7 @@
     recv, table, fits = exchange_and_analyse(
         obs_count.reshape(-1, GROUP), obs_ens, flat, obs_value, obs_weight
     )
+    recv = recv.reshape(HELD * WAYS, 32, LANES)
     result = scatter(table, flat, recv).reshape(members.shape)
     return lax.cond(
         fits[0, 0] > 0,

time: 55 us -> 53.8 us (0.978)
  Pallas kernels: 53.9 us -> 52.7 us
    pallas_call x1, Pallas kernels: 48.6 us -> 47.4 us  [exchange_and_analyse(): pl.pallas_call(analyse_kernel, out_shape=(jax.ShapeDtypeStruct((HELD, WAY...]
where the time goes in v5:
time: 53.8 us; the launch traced here: 53.5 us
  Pallas kernels  52.7 us (98%)
  between operations  0.84 us (2%)
    pallas_call x1, Pallas kernels, exchange_and_analyse(): pl.pallas_call(analyse_kernel, out_shape=(jax.ShapeDtypeStruct((HELD, WAY...  47.4 us
    pallas_call x1, Pallas kernels, scatter(): pl.pallas_call(scatter_kernel, out_shape=jax.ShapeDtypeStruct(members.sha...  5.27 us

profile of v5, /device:TPU:1, one launch (start us, length us, event | category | flops | bytes accessed | tf_op | source)
XLA Modules:
  0.0 53.5 jit_solution(12498487412890792995)
XLA Ops:
  0.0 0.0 copy-start
  0.0 47.4 %analyse.1 = (bf16[3,32,32,128]{3,2,1,0:T(8,128)(2,1)}, s32[40,128]{1,0:T(8,128)}, s32[1,1]{1,0:T(1,128)}) custom-call(s32[8,128]{1,0:T(8,128)} %bitcast.166, bf16[8,128,2048]{2,1,0:T(8,128)(2,1)} %obs_hbm.1, f32[4096,128]{1,0:T(8,128)} %bitcast.137, f32[4,2048]{1,0:T(4,128)} %values.1, f32[4,2048]{1,0:T(4,128)} %weights.1), custom_call_target="tpu_custom_call" | custom-call | tf_op jit(solution)/shard_map/analyse/pallas_call | solution.py:534
  47.4 0.0 copy-done
  47.4 0.0 copy-start.2
  47.4 0.0 copy-start.3
  47.4 5.3 %scatter.1 = f32[4096,128]{1,0:T(8,128)} custom-call(s32[40,128]{1,0:T(8,128)} %get-tuple-element.250.table, f32[4096,128]{1,0:T(8,128)S(1)} %bitcast.138, bf16[96,32,128]{2,1,0:T(8,128)(2,1)} %bitcast.147), custom_call_target="tpu_custom_call" | custom-call | tf_op jit(solution)/shard_map/scatter/pallas_call | solution.py:618
  53.3 0.0 copy-done.2
  53.3 0.0 copy-done.3
  (1 shorter events, 0.0 us)
Async XLA Ops:
  0.0 47.4 %copy-start = (f32[8,128,4,128]{3,2,1,0:T(4,128)S(1)}, f32[8,128,4,128]{3,2,1,0:T(4,128)}, u32[]{:S(2)}) copy-start(f32[8,128,4,128]{3,2,1,0:T(4,128)} %param.19) | copy-start | bytes 6291460
  47.4 5.9 %copy-start.2 = (f32[4,2048]{1,0:T(4,128)S(1)}, f32[4,2048]{1,0:T(4,128)}, u32[]{:S(2)}) copy-start(f32[4,2048]{1,0:T(4,128)} %values.1) | copy-start | bytes 98308
  47.4 5.9 %copy-start.3 = (f32[4,2048]{1,0:T(4,128)S(1)}, f32[4,2048]{1,0:T(4,128)}, u32[]{:S(2)}) copy-start(f32[4,2048]{1,0:T(4,128)} %weights.1) | copy-start | bytes 98308

commit v6 on v5

--- a/solution.py
+++ b/solution.py
@@ -120,7 +120,7 @@
     return lax.all_to_all(result, "ens", split_axis=0, concat_axis=1, tiled=True)
 
 
-def write_plan(counts, table, fits):
+def write_plan(counts, table):
     lane = lax.broadcasted_iota(jnp.int32, (8, LANES), 1)
     device = lane % WAYS
     tiles = counts[...]
@@ -152,7 +152,7 @@
         two = jnp.where(hit, pltpu.roll(second, step, 1) if step else second, two)
     load = blocks_of(one) + blocks_of(two) + blocks_of(third)
     over = (load > CAPACITY) | (blocks_of(third) > THIRD) | ((rank >= 80) & (tiles > 0))
-    fits[0, 0] = 1 - jnp.max(over.astype(jnp.int32))
+    over = jnp.max(jnp.max(over.astype(jnp.int32), axis=1, keepdims=True), axis=0, keepdims=True)
 
     row = lax.broadcasted_iota(jnp.int32, (8, LANES), 0)
     wide_lane = lax.broadcasted_iota(jnp.int32, (WAYS, LANES), 1)
@@ -193,7 +193,7 @@
     for slot in range(HELD):
         hit = (keys[slot] & (GROUP - 1) == wide_lane) & (size[slot] > 0)
         found += jnp.where(hit, slot * WAYS + wide_row + 1, 0)
-    table[WAYS : WAYS + 8, :] = jnp.broadcast_to(jnp.sum(found, axis=0, keepdims=True), (8, LANES))
+    table[WAYS : WAYS + 8, :] = jnp.where(row == 0, jnp.sum(found, axis=0, keepdims=True), 1 - over)
 
 
 def displacements():
@@ -246,9 +246,9 @@
 
 
 def analyse_kernel(
-    counts, obs_hbm, mem_hbm, values, weights,
-    out_recv, plan, fits,
-    table, obs_in, wide, mem_in, obs_send, mem_send, side_send, row_send, obs_recv, mem_recv,
+    counts_hbm, obs_hbm, mem_hbm, values_hbm, weights_hbm,
+    out_recv, plan_hbm, fits,
+    counts, values, weights, plan, table, obs_in, wide, mem_in, obs_send, mem_send, side_send, row_send, obs_recv, mem_recv,
     side_recv, row_recv, side, rows, out_send, root, root_t, pert,
     in_sem, phase_sem,
 ):
@@ -273,18 +273,27 @@
     obs_loads = [
         pltpu.make_async_copy(obs_hbm.at[m], obs_in.at[m], in_sem.at[m]) for m in range(ROWS)
     ]
-    for copy in obs_loads:
+    small_loads = [
+        pltpu.make_async_copy(values_hbm, values, in_sem.at[ROWS + 2]),
+        pltpu.make_async_copy(weights_hbm, weights, in_sem.at[ROWS + 3]),
+        pltpu.make_async_copy(counts_hbm, counts, in_sem.at[ROWS + 4]),
+    ]
+    for copy in small_loads + obs_loads:
         copy.start()
     mem_load.start()
+    for copy in small_loads:
+        copy.wait()
 
     parts = []
     for part in range(SLOT_BLOCKS):
         lanes = slice(part * LANES, (part + 1) * LANES)
         parts += [values[:, lanes] * CODE, jnp.sqrt(weights[:, lanes]) * ROOT_CODE]
     side_send[...] = coded(jnp.concatenate(parts, axis=0), 1.0)
-    write_plan(counts, plan, fits)
+    write_plan(counts, plan)
     table_copy = pltpu.make_async_copy(plan, table, in_sem.at[ROWS + 1])
     table_copy.start()
+    plan_copy = pltpu.make_async_copy(plan, plan_hbm, in_sem.at[ROWS + 5])
+    plan_copy.start()
     for m in range(ROWS):
         obs_loads[m].wait()
 
@@ -308,6 +317,8 @@
     pltpu.make_async_copy(side_send, side_recv.at[near], phase_sem.at[15]).start()
 
     table_copy.wait()
+    plan_copy.wait()
+    fits[0, 0] = table[WAYS + 1, 0]
 
     def pack_obs(dest, part):
         for pair in range(PART // 2):
@@ -527,8 +538,6 @@
 
 
 def exchange_and_analyse(counts, obs_ens, members, values, weights):
-    smem = pl.BlockSpec(memory_space=pltpu.SMEM)
-    vmem = pl.BlockSpec(memory_space=pltpu.VMEM)
     anywhere = pl.BlockSpec(memory_space=pl.ANY)
     dma = pltpu.SemaphoreType.DMA
     return pl.pallas_call(
@@ -538,9 +547,13 @@
             jax.ShapeDtypeStruct((WAYS + 8, LANES), jnp.int32),
             jax.ShapeDtypeStruct((1, 1), jnp.int32),
         ),
-        in_specs=[vmem, anywhere, anywhere, vmem, vmem],
-        out_specs=(anywhere, vmem, smem),
+        in_specs=[anywhere] * 5,
+        out_specs=(anywhere, anywhere, pl.BlockSpec(memory_space=pltpu.SMEM)),
         scratch_shapes=[
+            pltpu.VMEM((8, GROUP), jnp.int32),
+            pltpu.VMEM(values.shape, jnp.float32),
+            pltpu.VMEM(weights.shape, jnp.float32),
+            pltpu.VMEM((WAYS + 8, LANES), jnp.int32),
             pltpu.SMEM((WAYS + 8, LANES), jnp.int32),
             pltpu.VMEM((ROWS, GROUP, SLOT_BLOCKS * LANES), jnp.bfloat16),
             pltpu.VMEM((ROWS * SLOT_BLOCKS * GROUP, LANES), jnp.float32),
@@ -559,7 +572,7 @@
             pltpu.VMEM((ENS + 16, CAPACITY * LANES), jnp.bfloat16),
             pltpu.VMEM((CAPACITY * LANES, ENS), jnp.bfloat16),
             pltpu.VMEM((HELD, ENS, 4 * LANES), jnp.bfloat16),
-            dma((ROWS + 2,)),
+            dma((ROWS + 6,)),
             dma((20,)),
         ],
         compiler_params=pltpu.CompilerParams(
@@ -569,11 +582,12 @@
     )(counts, obs_ens, members, values, weights)
 
 
-def scatter_kernel(table, members, recv_hbm, out_hbm, recv, out, sems):
+def scatter_kernel(plan, members, recv_hbm, out_hbm, table, recv, out, sems):
     width = 4 * GROUP // CHUNKS
     recv_load = pltpu.make_async_copy(recv_hbm, recv, sems.at[0])
+    table_load = pltpu.make_async_copy(plan, table, sems.at[1 + 2 * CHUNKS])
+    table_load.start()
     recv_load.start()
-
     members = members.reshape(ROWS, 4 * GROUP, LANES)
     out_hbm = out_hbm.reshape(ROWS, 4 * GROUP, LANES)
 
@@ -581,62 +595,64 @@
         return pl.ds(chunk * width, width)
 
     loads = [
-        pltpu.make_async_copy(members.at[:, rows(c)], out.at[c], sems.at[1 + c])
+        pltpu.make_async_copy(
+            members.at[:, rows(c)], out.at[c, :, pl.ds(0, width)], sems.at[1 + c]
+        )
         for c in range(CHUNKS)
     ]
     stores = [
-        pltpu.make_async_copy(out.at[c], out_hbm.at[:, rows(c)], sems.at[1 + CHUNKS + c])
+        pltpu.make_async_copy(
+            out.at[c, :, pl.ds(0, width)], out_hbm.at[:, rows(c)], sems.at[1 + CHUNKS + c]
+        )
         for c in range(CHUNKS)
     ]
     for copy in loads:
         copy.start()
+    table_load.wait()
     recv_load.wait()
     for c in range(CHUNKS):
         loads[c].wait()
-        flat = out.at[c].reshape(ROWS * width, LANES)
+        flat = out.at[c].reshape(ROWS * (width + 8), LANES)
 
         def place(index, carry):
             at = table[WAYS, c * (GROUP // CHUNKS) + index]
-
-            @pl.when(at > 0)
-            def _():
-                tall = recv[at - 1].astype(jnp.float32)
-                for f in range(4):
-                    flat[pl.ds(index * 4 + f, ROWS, stride=width), :] = tall[f * ROWS : (f + 1) * ROWS]
-
+            tall = recv[jnp.maximum(at - 1, 0)].astype(jnp.float32)
+            row = jnp.where(at > 0, index * 4, width)
+            for f in range(4):
+                flat[pl.ds(row + f, ROWS, stride=width + 8), :] = tall[f * ROWS : (f + 1) * ROWS]
             return carry
 
-        lax.fori_loop(0, GROUP // CHUNKS, place, 0, unroll=4)
+        lax.fori_loop(0, GROUP // CHUNKS, place, 0, unroll=8)
         stores[c].start()
     for copy in stores:
         copy.wait()
 
 
-def scatter(table, members, recv):
-    smem = pl.BlockSpec(memory_space=pltpu.SMEM)
+def scatter(plan, members, recv):
     anywhere = pl.BlockSpec(memory_space=pl.ANY)
     return pl.pallas_call(
         scatter_kernel,
         out_shape=jax.ShapeDtypeStruct(members.shape, jnp.float32),
-        in_specs=[smem, anywhere, anywhere],
+        in_specs=[anywhere] * 3,
         out_specs=anywhere,
         scratch_shapes=[
+            pltpu.SMEM((WAYS + 8, LANES), jnp.int32),
             pltpu.VMEM(recv.shape, recv.dtype),
-            pltpu.VMEM((CHUNKS, ROWS, 4 * GROUP // CHUNKS, LANES), jnp.float32),
-            pltpu.SemaphoreType.DMA((1 + 2 * CHUNKS,)),
+            pltpu.VMEM((CHUNKS, ROWS, 4 * GROUP // CHUNKS + 8, LANES), jnp.float32),
+            pltpu.SemaphoreType.DMA((2 + 2 * CHUNKS,)),
         ],
         compiler_params=pltpu.CompilerParams(vmem_limit_bytes=60 << 20),
         name="scatter",
-    )(table, members, recv)
+    )(plan, members, recv)
 
 
 def body(members, obs_ens, obs_count, obs_value, obs_weight):
     flat = members.reshape(-1, LANES)
-    recv, table, fits = exchange_and_analyse(
+    recv, plan, fits = exchange_and_analyse(
         obs_count.reshape(-1, GROUP), obs_ens, flat, obs_value, obs_weight
     )
     recv = recv.reshape(HELD * WAYS, 32, LANES)
-    result = scatter(table, flat, recv).reshape(members.shape)
+    result = scatter(plan, flat, recv).reshape(members.shape)
     return lax.cond(
         fits[0, 0] > 0,
         lambda result, *_: result,

time: 53.8 us -> 50.5 us (0.939)
  Pallas kernels: 52.7 us -> 49.5 us
    pallas_call x1, Pallas kernels: 5.27 us -> 2.9 us  [scatter(): pl.pallas_call(scatter_kernel, out_shape=jax.ShapeDtypeStruct(members.sha...]
    pallas_call x1, Pallas kernels: 47.4 us -> 46.6 us  [exchange_and_analyse(): pl.pallas_call(analyse_kernel, out_shape=(jax.ShapeDtypeStruct((HELD, WAY...]
where the time goes in v6:
time: 50.5 us; the launch traced here: 50.4 us
  Pallas kernels  49.5 us (98%)
  between operations  0.84 us (2%)
    pallas_call x1, Pallas kernels, exchange_and_analyse(): pl.pallas_call(analyse_kernel, out_shape=(jax.ShapeDtypeStruct((HELD, WAY...  46.6 us
    pallas_call x1, Pallas kernels, scatter(): pl.pallas_call(scatter_kernel, out_shape=jax.ShapeDtypeStruct(members.sha...  2.9 us

profile of v6, /device:TPU:1, one launch (start us, length us, event | category | flops | bytes accessed | tf_op | source)
XLA Modules:
  0.0 50.4 jit_solution(6024851910443130244)
XLA Ops:
  0.0 0.0 copy-start
  0.0 46.6 %analyse.1 = (bf16[3,32,32,128]{3,2,1,0:T(8,128)(2,1)}, s32[40,128]{1,0:T(8,128)}, s32[1,1]{1,0:T(1,128)}) custom-call(s32[8,128]{1,0:T(8,128)} %bitcast.166, bf16[8,128,2048]{2,1,0:T(8,128)(2,1)} %obs_hbm.1, f32[4096,128]{1,0:T(8,128)} %bitcast.137, f32[4,2048]{1,0:T(4,128)} %values_hbm.1, f32[4,2048]{1,0:T(4,128)} %weights_hbm.1), custom_call_target="tpu_custom_call" | custom-call | tf_op jit(solution)/shard_map/analyse/pallas_call | solution.py:543
  46.6 0.0 copy-done
  46.6 0.0 copy-start.2
  46.6 0.0 copy-start.3
  46.6 2.9 %scatter.1 = f32[4096,128]{1,0:T(8,128)} custom-call(s32[40,128]{1,0:T(8,128)} %get-tuple-element.250.plan, f32[4096,128]{1,0:T(8,128)S(1)} %bitcast.138, bf16[96,32,128]{2,1,0:T(8,128)(2,1)} %bitcast.147), custom_call_target="tpu_custom_call" | custom-call | tf_op jit(solution)/shard_map/scatter/pallas_call | solution.py:633
  50.2 0.0 copy-done.2
  50.2 0.0 copy-done.3
  (1 shorter events, 0.0 us)
Async XLA Ops:
  0.0 46.6 %copy-start = (f32[8,128,4,128]{3,2,1,0:T(4,128)S(1)}, f32[8,128,4,128]{3,2,1,0:T(4,128)}, u32[]{:S(2)}) copy-start(f32[8,128,4,128]{3,2,1,0:T(4,128)} %param.19) | copy-start | bytes 6291460
  46.6 3.6 %copy-start.2 = (f32[4,2048]{1,0:T(4,128)S(1)}, f32[4,2048]{1,0:T(4,128)}, u32[]{:S(2)}) copy-start(f32[4,2048]{1,0:T(4,128)} %values_hbm.1) | copy-start | bytes 98308
  46.6 3.6 %copy-start.3 = (f32[4,2048]{1,0:T(4,128)S(1)}, f32[4,2048]{1,0:T(4,128)}, u32[]{:S(2)}) copy-start(f32[4,2048]{1,0:T(4,128)} %weights_hbm.1) | copy-start | bytes 98308

commit v7 on v6

--- a/solution.py
+++ b/solution.py
@@ -15,7 +15,7 @@
 SLOT_BLOCKS = 16
 HELD = 3
 CAPACITY = 24
-PART = 12
+PARTS = (0, 10, 20, 24)
 THIRD = 6
 CHUNKS = 4
 ROWS = 8
@@ -120,7 +120,7 @@
     return lax.all_to_all(result, "ens", split_axis=0, concat_axis=1, tiled=True)
 
 
-def write_plan(counts, table):
+def write_plan(counts, table, fits):
     lane = lax.broadcasted_iota(jnp.int32, (8, LANES), 1)
     device = lane % WAYS
     tiles = counts[...]
@@ -193,7 +193,8 @@
     for slot in range(HELD):
         hit = (keys[slot] & (GROUP - 1) == wide_lane) & (size[slot] > 0)
         found += jnp.where(hit, slot * WAYS + wide_row + 1, 0)
-    table[WAYS : WAYS + 8, :] = jnp.where(row == 0, jnp.sum(found, axis=0, keepdims=True), 1 - over)
+    table[WAYS : WAYS + 8, :] = jnp.broadcast_to(jnp.sum(found, axis=0, keepdims=True), (8, LANES))
+    fits[...] = 1 - over
 
 
 def displacements():
@@ -247,13 +248,16 @@
 
 def analyse_kernel(
     counts_hbm, obs_hbm, mem_hbm, values_hbm, weights_hbm,
-    out_recv, plan_hbm, fits,
-    counts, values, weights, plan, table, obs_in, wide, mem_in, obs_send, mem_send, side_send, row_send, obs_recv, mem_recv,
+    out_recv, plan_hbm, fits_hbm,
+    counts, values, weights, plan, fits, table, obs_in, wide, mem_in, obs_send_a, obs_send_b, obs_send_c, mem_send, side_send,
+    row_send, obs_recv_a, obs_recv_b, obs_recv_c, mem_recv,
     side_recv, row_recv, side, rows, out_send, root, root_t, pert,
-    in_sem, phase_sem,
+    in_sem, phase_sem, obs_sem,
 ):
     me = lax.axis_index("ens")
     core = me % 2
+    obs_send = (obs_send_a, obs_send_b, obs_send_c)
+    obs_recv = (obs_recv_a, obs_recv_b, obs_recv_c)
     steps = displacements()
     targets = [shifted(me, step) for step in steps]
 
@@ -289,11 +293,13 @@
         lanes = slice(part * LANES, (part + 1) * LANES)
         parts += [values[:, lanes] * CODE, jnp.sqrt(weights[:, lanes]) * ROOT_CODE]
     side_send[...] = coded(jnp.concatenate(parts, axis=0), 1.0)
-    write_plan(counts, plan)
+    write_plan(counts, plan, fits)
     table_copy = pltpu.make_async_copy(plan, table, in_sem.at[ROWS + 1])
     table_copy.start()
     plan_copy = pltpu.make_async_copy(plan, plan_hbm, in_sem.at[ROWS + 5])
     plan_copy.start()
+    fits_copy = pltpu.make_async_copy(fits, fits_hbm, in_sem.at[ROWS + 6])
+    fits_copy.start()
     for m in range(ROWS):
         obs_loads[m].wait()
 
@@ -318,27 +324,27 @@
 
     table_copy.wait()
     plan_copy.wait()
-    fits[0, 0] = table[WAYS + 1, 0]
+    fits_copy.wait()
 
     def pack_obs(dest, part):
-        for pair in range(PART // 2):
-            at = part * PART + 2 * pair
+        for pair in range((PARTS[part + 1] - PARTS[part]) // 2):
+            at = PARTS[part] + 2 * pair
             rows = [
                 wide[pl.ds(table[dest, at + j], ROWS, stride=SLOT_BLOCKS * GROUP), :]
                 for j in range(2)
             ]
-            obs_send[part, dest, pair] = jnp.concatenate(rows, axis=0).astype(jnp.bfloat16)
+            obs_send[part][dest, pair] = jnp.concatenate(rows, axis=0).astype(jnp.bfloat16)
 
     def send_obs(part):
         for target in targets:
             pack_obs(target, part)
             remote(
-                obs_send.at[part, target], obs_recv.at[part, me],
-                phase_sem.at[part], phase_sem.at[16 + part], target,
+                obs_send[part].at[target], obs_recv[part].at[me],
+                obs_sem.at[part], obs_sem.at[3 + part], target,
             ).start()
         pack_obs(me, part)
         pltpu.make_async_copy(
-            obs_send.at[part, me], obs_recv.at[part, me], phase_sem.at[16 + part]
+            obs_send[part].at[me], obs_recv[part].at[me], obs_sem.at[3 + part]
         ).start()
 
     def pack_members(dest, slot):
@@ -370,6 +376,7 @@
                 ).start()
 
     send_obs(1)
+    send_obs(2)
 
     mem_load.wait()
     for slot in range(HELD):
@@ -403,10 +410,11 @@
     lane = lax.broadcasted_iota(jnp.int32, (1, LANES), 1)
 
     def form_roots(block):
-        part, place = block // PART, block % PART
+        part = sum(block >= begin for begin in PARTS[1:-1])
+        place = block - PARTS[part]
         half = (place % 2) * ROWS
         columns = pl.ds(block * LANES, LANES)
-        seen = obs_recv[part, :, place // 2].astype(jnp.float32)[:, half : half + ROWS, :]
+        seen = obs_recv[part][:, place // 2].astype(jnp.float32)[:, half : half + ROWS, :]
         seen = seen.reshape(ENS, LANES)
         mean = jnp.sum(seen, axis=0, keepdims=True) * (1.0 / ENS)
         owner = (table[me, block] & (GROUP - 1)) >> 2
@@ -436,7 +444,7 @@
     held = range(HELD)
 
     def sums_of(slot, part):
-        low, high = max(reach[slot][0], part * PART), min(reach[slot][1], (part + 1) * PART)
+        low, high = max(reach[slot][0], PARTS[part]), min(reach[slot][1], PARTS[part + 1])
         if low >= high:
             return None
         place = low + lax.broadcasted_iota(jnp.int32, (1, (high - low) * LANES), 1) // LANES
@@ -446,13 +454,14 @@
             masked, root_t[low * LANES : high * LANES, :], preferred_element_type=jnp.float32
         )
 
-    drain(obs_recv.at[0], phase_sem.at[16])
-    for block in range(PART):
-        form_roots(block)
-    early = [sums_of(slot, 0) for slot in held]
-    drain(obs_recv.at[1], phase_sem.at[17])
-    for block in range(PART, CAPACITY):
-        form_roots(block)
+    sums = [None] * HELD
+    for part in range(len(PARTS) - 1):
+        drain(obs_recv[part], obs_sem.at[3 + part])
+        for block in range(PARTS[part], PARTS[part + 1]):
+            form_roots(block)
+        for slot in held:
+            more = sums_of(slot, part)
+            sums[slot] = more if sums[slot] is None else sums[slot] if more is None else sums[slot] + more
 
     def centre_members(slot):
         if slot < 2:
@@ -469,11 +478,8 @@
     def weights_of(slots):
         vecs, bounds, ys, means = [], [], [], []
         for slot in slots:
-            sums = sums_of(slot, 1)
-            if early[slot] is not None:
-                sums = sums + early[slot]
-            gram = sums[0:ENS]
-            vecs.append(sums[ENS : ENS + 8])
+            gram = sums[slot][0:ENS]
+            vecs.append(sums[slot][ENS : ENS + 8])
             trace = jnp.sum((gram[:half, :half] + gram[half:, half:]) * eye)
             bound = (ENS - 1.0) + trace
             bounds.append(bound)
@@ -523,8 +529,8 @@
                 pl.when(core == 0)(send_result)
 
     sent = pl.ds(0, WAYS - 1)
-    for part in range(2):
-        drain(obs_send.at[part, sent], phase_sem.at[part])
+    for part in range(len(PARTS) - 1):
+        drain(obs_send[part].at[sent], obs_sem.at[part])
     drain(side_recv.at[pl.ds(0, 3)], phase_sem.at[14])
     drain(row_send.at[pl.ds(0, 7)], phase_sem.at[18])
     for slot in range(2):
@@ -540,6 +546,10 @@
 def exchange_and_analyse(counts, obs_ens, members, values, weights):
     anywhere = pl.BlockSpec(memory_space=pl.ANY)
     dma = pltpu.SemaphoreType.DMA
+    obs_parts = [
+        pltpu.VMEM((WAYS, (end - begin) // 2, 16, LANES), jnp.bfloat16)
+        for begin, end in zip(PARTS, PARTS[1:])
+    ]
     return pl.pallas_call(
         analyse_kernel,
         out_shape=(
@@ -548,21 +558,22 @@
             jax.ShapeDtypeStruct((1, 1), jnp.int32),
         ),
         in_specs=[anywhere] * 5,
-        out_specs=(anywhere, anywhere, pl.BlockSpec(memory_space=pltpu.SMEM)),
+        out_specs=(anywhere, anywhere, anywhere),
         scratch_shapes=[
             pltpu.VMEM((8, GROUP), jnp.int32),
             pltpu.VMEM(values.shape, jnp.float32),
             pltpu.VMEM(weights.shape, jnp.float32),
             pltpu.VMEM((WAYS + 8, LANES), jnp.int32),
+            pltpu.VMEM((1, 1), jnp.int32),
             pltpu.SMEM((WAYS + 8, LANES), jnp.int32),
             pltpu.VMEM((ROWS, GROUP, SLOT_BLOCKS * LANES), jnp.bfloat16),
             pltpu.VMEM((ROWS * SLOT_BLOCKS * GROUP, LANES), jnp.float32),
             pltpu.VMEM((ROWS * GROUP * 4, LANES), jnp.float32),
-            pltpu.VMEM((2, WAYS, PART // 2, 16, LANES), jnp.bfloat16),
+            *obs_parts,
             pltpu.VMEM((HELD, WAYS, 32, LANES), jnp.int16),
             pltpu.VMEM((SIDE_ROWS, LANES), jnp.int16),
             pltpu.VMEM((8, 2 * CAPACITY, LANES), jnp.int16),
-            pltpu.VMEM((2, WAYS, PART // 2, 16, LANES), jnp.bfloat16),
+            *obs_parts,
             pltpu.VMEM((HELD, WAYS, 32, LANES), jnp.int16),
             pltpu.VMEM((4, SIDE_ROWS, LANES), jnp.int16),
             pltpu.VMEM((8, 2 * CAPACITY, LANES), jnp.int16),
@@ -572,8 +583,9 @@
             pltpu.VMEM((ENS + 16, CAPACITY * LANES), jnp.bfloat16),
             pltpu.VMEM((CAPACITY * LANES, ENS), jnp.bfloat16),
             pltpu.VMEM((HELD, ENS, 4 * LANES), jnp.bfloat16),
-            dma((ROWS + 6,)),
+            dma((ROWS + 7,)),
             dma((20,)),
+            dma((6,)),
         ],
         compiler_params=pltpu.CompilerParams(
             collective_id=0, has_side_effects=True, vmem_limit_bytes=56 << 20

time: 50.5 us -> 49.9 us (0.988)
  Pallas kernels: 49.5 us -> 48.9 us
    pallas_call x1, Pallas kernels: 46.6 us -> 46 us  [exchange_and_analyse(): pl.pallas_call(analyse_kernel, out_shape=(jax.ShapeDtypeStruct((HELD, WAY...]
where the time goes in v7:
time: 49.9 us; the launch traced here: 49.8 us
  Pallas kernels  48.9 us (98%)
  between operations  0.84 us (2%)
    pallas_call x1, Pallas kernels, exchange_and_analyse(): pl.pallas_call(analyse_kernel, out_shape=(jax.ShapeDtypeStruct((HELD, WAY...  46 us
    pallas_call x1, Pallas kernels, scatter(): pl.pallas_call(scatter_kernel, out_shape=jax.ShapeDtypeStruct(members.sha...  2.9 us

profile of v7, /device:TPU:1, one launch (start us, length us, event | category | flops | bytes accessed | tf_op | source)
XLA Modules:
  0.0 49.8 jit_solution(17632586913771656091)
XLA Ops:
  0.0 0.0 copy-start
  0.0 46.0 %analyse.1 = (bf16[3,32,32,128]{3,2,1,0:T(8,128)(2,1)}, s32[40,128]{1,0:T(8,128)}, s32[1,1]{1,0:T(1,128)}) custom-call(s32[8,128]{1,0:T(8,128)} %bitcast.166, bf16[8,128,2048]{2,1,0:T(8,128)(2,1)} %obs_hbm.1, f32[4096,128]{1,0:T(8,128)} %bitcast.137, f32[4,2048]{1,0:T(4,128)} %values_hbm.1, f32[4,2048]{1,0:T(4,128)} %weights_hbm.1), custom_call_target="tpu_custom_call" | custom-call | tf_op jit(solution)/shard_map/analyse/pallas_call | solution.py:553
  46.0 0.0 copy-done
  46.0 0.0 copy-start.2
  46.0 0.0 copy-start.3
  46.0 2.9 %scatter.1 = f32[4096,128]{1,0:T(8,128)} custom-call(s32[40,128]{1,0:T(8,128)} %get-tuple-element.250.plan, f32[4096,128]{1,0:T(8,128)S(1)} %bitcast.138, bf16[96,32,128]{2,1,0:T(8,128)(2,1)} %bitcast.147), custom_call_target="tpu_custom_call" | custom-call | tf_op jit(solution)/shard_map/scatter/pallas_call | solution.py:645
  49.6 0.0 copy-done.2
  49.6 0.0 copy-done.3
  (1 shorter events, 0.0 us)
Async XLA Ops:
  0.0 46.0 %copy-start = (f32[8,128,4,128]{3,2,1,0:T(4,128)S(1)}, f32[8,128,4,128]{3,2,1,0:T(4,128)}, u32[]{:S(2)}) copy-start(f32[8,128,4,128]{3,2,1,0:T(4,128)} %param.19) | copy-start | bytes 6291460
  46.0 3.6 %copy-start.2 = (f32[4,2048]{1,0:T(4,128)S(1)}, f32[4,2048]{1,0:T(4,128)}, u32[]{:S(2)}) copy-start(f32[4,2048]{1,0:T(4,128)} %values_hbm.1) | copy-start | bytes 98308
  46.0 3.6 %copy-start.3 = (f32[4,2048]{1,0:T(4,128)S(1)}, f32[4,2048]{1,0:T(4,128)}, u32[]{:S(2)}) copy-start(f32[4,2048]{1,0:T(4,128)} %weights_hbm.1) | copy-start | bytes 98308
